TPU v7x, 32 devices: a whole 2x2x4 slice. The times are simulated.
32 devices in a mesh: dp: 8 (over z, y), head: 4 (over x, core).
Axes of the slice: x: 2, y: 2, z: 4, core: 2. Of those that a mesh axis runs over, the one named last changes fastest.
Arguments:
- hidden_input: bfloat16 [40, 512, 768], P('dp'), may hold values from -6 to 6
- grad_out: bfloat16 [40, 512, 768], P('dp', 'head'), may hold values from -6 to 6
- pair_lengths: int32 [40], P('dp'), may hold values from 64 to 512, as said below
- query_key_value_weight: bfloat16 [3, 768, 768], P(None, None, 'head'), may hold values from -0.21875 to 0.21875
- qkv_bias: float32 [3, 768], replicated, may hold values from -4 to 4
- output_projection_weight: bfloat16 [768, 768], P('head'), may hold values from -0.875 to 0.875
- shifts: float32 [4, 768], replicated, may hold values from -4 to 4
- gains: float32 [2, 768], replicated, may hold values from 0.5 to 1.5
- up_projection_weight: bfloat16 [768, 3072], P(None, 'head'), may hold values from -0.21875 to 0.21875
- up_bias: float32 [3072], replicated, may hold values from -4 to 4
- down_projection_weight: bfloat16 [3072, 768], P('head'), may hold values from -0.109375 to 0.109375
- adapters_model: float32 [10, 768, 16], P(None, ('dp', 'head'))
- adapters_inner: float32 [2, 3072, 16], P(None, ('dp', 'head'))
- stats_model: float32 [10, 768, 768], P(None, ('dp', 'head')), as said below
- stats_inner: float32 [2, 3072, 3072], P(None, ('dp', 'head')), as said below
- stats_rank: float32 [12, 16, 16], replicated, as said below
- roots_model: float32 [10, 768, 768], P(None, ('dp', 'head'))
- roots_inner: float32 [2, 3072, 3072], P(None, ('dp', 'head'))
- roots_rank: float32 [12, 16, 16], replicated
Outputs:
- hidden_out: bfloat16 [40, 512, 768], P('dp', 'head')
- grad_in: bfloat16 [40, 512, 768], P('dp', 'head')
- grads_model: float32 [10, 768, 16], P(None, ('dp', 'head'))
- grads_inner: float32 [2, 3072, 16], P(None, ('dp', 'head'))
- adapters_model_new: float32 [10, 768, 16], P(None, ('dp', 'head'))
- adapters_inner_new: float32 [2, 3072, 16], P(None, ('dp', 'head'))
- stats_model_new: float32 [10, 768, 768], P(None, ('dp', 'head'))
- stats_inner_new: float32 [2, 3072, 3072], P(None, ('dp', 'head'))
- stats_rank_new: float32 [12, 16, 16], replicated
Inputs may be any that keep to these rules, and one draw needn't show every extreme that they name: `pair_lengths`: a pair's tokens come first in its slot and padding follows; some pair fills its whole slot. `stats_model`: each matrix is symmetric. `stats_inner`: each matrix is symmetric. `stats_rank`: each matrix is symmetric.
All inputs are finite; a program needn't handle non-finite values.
Results may differ from a plain program's by a relative error of at most 0.024.
Values may be sent and summed in bfloat16 or wider, within the bound.
A program may use at most 128 MiB of HBM per device.

v0:
```python
import functools

import jax
import jax.numpy as jnp
from jax import lax
from jax.experimental import pallas as pl
from jax.experimental.pallas import tpu as pltpu
from jax.sharding import PartitionSpec as P

DH = 64
RANK = 16
LANES = 128
LOWRANK = 2.0
RATE_FIRST = 0.01
RATE_SECOND = 0.16
DECAY = 0.5
EPS_NORM = 1e-5
MESH = pl.DeviceIdType.MESH
VMEM_LIMIT = 60 << 20
F32 = jnp.float32
BF16 = jnp.bfloat16
HIGH = lax.Precision.HIGHEST

EARLY_SLOTS = (0, 1, 2, 5, 6, 7)
LATE_SLOTS = (3, 4, 8, 9)


def slot_of(j):
    if j in EARLY_SLOTS:
        return 0, EARLY_SLOTS.index(j)
    return 1, LATE_SLOTS.index(j)


def nn(a, b, precision=None):
    return lax.dot_general(
        a, b, (((1,), (0,)), ((), ())), precision=precision, preferred_element_type=F32
    )


def nt(a, b, precision=None):
    return lax.dot_general(
        a, b, (((1,), (1,)), ((), ())), precision=precision, preferred_element_type=F32
    )


def tn(a, b, precision=None):
    return lax.dot_general(
        a, b, (((0,), (0,)), ((), ())), precision=precision, preferred_element_type=F32
    )


def vmem():
    return pl.BlockSpec(memory_space=pltpu.VMEM)


def anywhere():
    return pl.BlockSpec(memory_space=pl.ANY)


def greet_signal(nd, nh):
    d, h = lax.axis_index("dp"), lax.axis_index("head")
    barrier = pltpu.get_barrier_semaphore()
    for k in range(1, nd):
        pl.semaphore_signal(
            barrier, inc=1, device_id=(lax.rem(d + k, nd), h), device_id_type=MESH
        )
    for k in range(1, nh):
        pl.semaphore_signal(
            barrier, inc=1, device_id=(d, lax.rem(h + k, nh)), device_id_type=MESH
        )


def greet_wait(nd, nh):
    pl.semaphore_wait(pltpu.get_barrier_semaphore(), nd + nh - 2)


def greet(nd, nh):
    greet_signal(nd, nh)
    greet_wait(nd, nh)


def remote(src, dst, send, recv, device):
    return pltpu.make_async_remote_copy(
        src, dst, send, recv, device_id=device, device_id_type=MESH
    )


class Reduction:
    def __init__(self, nd, nh, bufs, sems):
        self.nd, self.nh = nd, nh
        self.out, self.part, self.near, self.full = bufs
        self.sems = sems
        self.d, self.h = lax.axis_index("dp"), lax.axis_index("head")

    @staticmethod
    def scratch(nd, nh, tiles, model):
        rows = -(-(model // nd) // 16) * 16
        dma = pltpu.SemaphoreType.DMA
        return (
            [
                pltpu.VMEM((nd, tiles, rows, LANES), BF16),
                pltpu.VMEM((nd, tiles, rows, LANES), BF16),
                pltpu.VMEM((4, tiles, rows, LANES), BF16),
                pltpu.VMEM((nd, tiles, rows, LANES), BF16),
            ],
            [dma((nd,)), dma((nd,)), dma((2,)), dma((2,)), dma((nd,)), dma((nd,))],
        )

    def to_owner(self, k):
        peer = lax.rem(self.d + k, self.nd)
        return remote(
            self.out.at[peer], self.part.at[k], self.sems[0].at[k], self.sems[1].at[k],
            (peer, self.h),
        )

    def across(self, i):
        return remote(
            self.near.at[2 * i], self.near.at[2 * i + 1], self.sems[2].at[i],
            self.sems[3].at[i], (self.d, jnp.bitwise_xor(self.h, i + 1)),
        )

    def to_all(self, k):
        here = self.full.at[self.d]
        return remote(
            here, here, self.sems[4].at[k], self.sems[5].at[k],
            (lax.rem(self.d + k, self.nd), self.h),
        )

    def start(self, values):
        size = values.shape[1] // self.nd
        for i in range(self.nd):
            self.out[i, :, 0:size] = values[:, i * size : (i + 1) * size].astype(BF16)
        for k in range(1, self.nd):
            self.to_owner(k).start()

    def over_dp(self):
        total = self.out[self.d].astype(F32)
        for k in range(1, self.nd):
            self.to_owner(k).wait_recv()
            total = total + self.part[k].astype(F32)
        self.near[0] = total.astype(BF16)
        self.across(0).start()

    def over_head(self, i):
        self.across(i).wait_recv()
        total = self.near[2 * i].astype(F32) + self.near[2 * i + 1].astype(F32)
        if i == 0:
            self.near[2] = total.astype(BF16)
            self.across(1).start()
        else:
            self.full[self.d] = total.astype(BF16)
            for k in range(1, self.nd):
                self.to_all(k).start()

    def finish(self, target):
        size = target.shape[1] // self.nd
        for k in range(1, self.nd):
            self.to_all(k).wait_recv()
        for i in range(self.nd):
            target[:, i * size : (i + 1) * size] = self.full[i, :, 0:size].astype(F32)
        for k in range(1, self.nd):
            self.to_owner(k).wait_send()
            self.to_all(k).wait_send()
        for i in range(2):
            self.across(i).wait_send()


def attend_kernel(
    nd, nh, lengths, am, ai, x_hbm, w_ref, bias_ref, wo, wu, wd,
    proj_ref, p_ref, inv_ref, o_all, go_w, gu_w, gd_w, wt, tile_a, bt, down_t,
    packed, first_tile, other_tiles, obuf, bias_col, unpack, x_ref, raw, up_t, pt,
    load_x,
    send_d, recv_d, send_h, recv_h, send_o, recv_o, keep_o, send_w, recv_w, send_s, recv_s,
):
    step = pl.program_id(0)
    d, h = lax.axis_index("dp"), lax.axis_index("head")
    count, keys, model = x_ref.shape
    part = keys // nh
    width = w_ref.shape[1]
    rows = am.shape[2]
    split = ai.shape[2] // rows
    owners = nd * nh
    quarter = lax.rem(d, 4)

    def at(a, b):
        return (jnp.bitwise_xor(d, a), jnp.bitwise_xor(h, b))

    own_w = (wo, wu, wd)
    all_w = (go_w, gu_w, gd_w)
    chunks = []
    for w in range(3):
        quarter_rows = own_w[w].shape[0] // 4
        pieces = 1 if w == 0 else 2
        for piece in range(pieces):
            chunks.append((w, quarter_rows, piece * quarter_rows // pieces, quarter_rows // pieces))

    def region(ref, c, who, half=None):
        w, quarter_rows, offset, size = chunks[c]
        base = jnp.bitwise_xor(quarter, who) * quarter_rows + offset
        if half is not None:
            first = -(-(size // 2) // 16) * 16
            base, size = (base, first) if half == 0 else (base + first, size - first)
        return ref.at[pl.ds(pl.multiple_of(base, 16), size)]

    def over_x(c):
        w = chunks[c][0]
        return remote(
            region(own_w[w], c, 0), region(all_w[w].at[1], c, 0),
            send_w.at[0, c], recv_w.at[0, c], at(0, 2),
        )

    def spread_w(c, axis):
        here = region(all_w[chunks[c][0]].at[1], c, 0)
        return remote(here, here, send_w.at[axis, c], recv_w.at[axis, c], at(axis, 0))

    def relay_w(c, axis):
        here = region(all_w[chunks[c][0]].at[1], c, 3 - axis, axis - 1)
        return remote(here, here, send_w.at[2 + axis, c], recv_w.at[2 + axis, c], at(axis, 0))

    def sibling_own(w):
        return remote(own_w[w], all_w[w].at[0], send_s.at[0, w], recv_s.at[0, w], at(0, 1))

    def sibling_far(w):
        return remote(
            all_w[w].at[1], all_w[w].at[2], send_s.at[1, w], recv_s.at[1, w], at(0, 1)
        )

    def forward(c):
        over_x(c).wait_recv()
        spread_w(c, 2).start()
        spread_w(c, 1).start()

    def relay(c):
        spread_w(c, 2).wait_recv()
        relay_w(c, 1).start()
        spread_w(c, 1).wait_recv()
        relay_w(c, 2).start()

    def arrived(c):
        relay_w(c, 1).wait_recv()
        relay_w(c, 2).wait_recv()

    def finish(w, which):
        for c in which:
            arrived(c)
        sibling_far(w).start()

    stores = (first_tile, other_tiles)
    sources = (packed.at[pl.ds(0, 1)], packed.at[pl.ds(1, 2)])
    critical, later = 0, 1

    def to_dp(k, slot):
        return remote(
            sources[slot], stores[slot].at[h, d], send_d.at[slot, k], recv_d.at[slot, k],
            (lax.rem(d + k, nd), h),
        )

    def to_head(b, slot):
        column = stores[slot].at[h]
        return remote(column, column, send_h.at[slot, b], recv_h.at[slot, b], at(0, b))

    def pass_on(slot):
        column = stores[slot].at[jnp.bitwise_xor(h, 2)]
        return remote(column, column, send_h.at[slot, 3], recv_h.at[slot, 3], at(0, 1))

    def entry(t, owner):
        if t == 0:
            return first_tile[owner % nh, owner // nh, 0, 0:rows]
        return other_tiles[owner % nh, owner // nh, t - 1, 0:rows]

    def natural(t):
        return jnp.concatenate([entry(t, i) for i in range(owners)], axis=0)

    def fetch_x(i):
        return pltpu.make_async_copy(x_hbm.at[i], x_ref.at[i], load_x.at[i])

    def project(i):
        fetch_x(i).wait()
        for j in range(3):
            raw[i, j * width : (j + 1) * width] = nt(w_ref[j], x_ref[i])

    @pl.when(step == 0)
    def _():
        for i in range(count):
            fetch_x(i).start()
        greet_signal(nd, nh)
        packed[...] = jnp.zeros_like(packed)
        groups = [
            [am[j] for j in EARLY_SLOTS],
            [am[j] for j in LATE_SLOTS],
            [ai[q][:, k * rows : (k + 1) * rows] for k in range(split) for q in range(2)],
        ]
        for t, group in enumerate(groups):
            short = LANES - len(group) * RANK
            if short:
                group = group + [jnp.zeros((short, rows), F32)]
            packed[t, 0:rows] = jnp.concatenate(group, axis=0).T.astype(BF16).astype(F32)
        first_tile[h, d] = packed[0:1]
        other_tiles[h, d] = packed[1:3]
        project(0)
        greet_wait(nd, nh)
        for k in range(1, nd):
            to_dp(k, critical).start()
        over_x(0).start()
        over_x(1).start()
        project(1)
        project(2)
        for k in range(1, nd):
            to_dp(k, critical).wait_recv()
        to_head(2, critical).start()
        to_head(1, critical).start()
        for c in range(2, len(chunks)):
            over_x(c).start()
        project(3)
        to_head(2, critical).wait_recv()
        pass_on(critical).start()
        sibling_own(0).start()
        sibling_own(1).start()
        sibling_own(2).start()
        project(4)
        bias_col[...] = jnp.concatenate(
            [bias_ref[...], jnp.zeros((5, model), F32)], axis=0
        ).T
        to_head(1, critical).wait_recv()
        pass_on(critical).wait_recv()
        pn = natural(0)
        pt[...] = pn.T.astype(BF16)
        tile_a[...] = pn
        own = tile_a[pl.ds(pl.multiple_of(h * width, width), width), :]
        down_t[...] = own.T.astype(BF16)
        own = own[:, 3 * RANK : 6 * RANK].astype(BF16)
        lane = lax.broadcasted_iota(jnp.int32, own.shape, 1)
        for j in range(3):
            inside = (lane >= j * RANK) & (lane < (j + 1) * RANK)
            up_t[j * width : (j + 1) * width] = jnp.where(inside, own, jnp.zeros_like(own))
        for k in range(1, nd):
            to_dp(k, later).start()

    inner = nt(pt[0 : 3 * RANK], x_ref[step]).astype(BF16)
    proj_ref[0, 3 * width :] = inner
    mine = pl.ds(pl.multiple_of(h * width, width), width)
    for j in range(3):
        part_j = slice(j * width, (j + 1) * width)
        proj_ref[0, part_j] = (
            raw[step, part_j] + LOWRANK * nn(up_t[part_j], inner) + bias_col[mine, j : j + 1]
        ).astype(BF16)
    valid = lax.broadcasted_iota(jnp.int32, (keys, 1), 0) < lengths[step]

    def slot(s, place):
        for action in plan.get((s, place), ()):
            action()

    def slots(place):
        for s in range(count):
            if (s, place) in plan:
                pl.when(step == s)(functools.partial(slot, s, place))

    def later_to_head():
        for k in range(1, nd):
            to_dp(k, later).wait_recv()
        to_head(2, later).start()
        to_head(1, later).start()

    def later_pass_on():
        to_head(2, later).wait_recv()
        pass_on(later).start()

    bind = functools.partial
    plan = {
        (0, 0): [bind(forward, 0)],
        (0, 1): [bind(forward, 1)],
        (1, 1): [bind(forward, 2), bind(relay, 0)],
        (1, 3): [later_to_head, bind(relay, 1)],
        (2, 1): [bind(forward, 3)],
        (2, 3): [bind(forward, 4), bind(relay, 2)],
        (3, 1): [bind(relay, 3), bind(finish, 0, (0,))],
        (3, 3): [later_pass_on, bind(relay, 4)],
        (4, 1): [bind(finish, 1, (1, 2))],
    }

    results = []
    for head in range(width // DH):
        slots(head)
        rows_q = slice(head * DH, (head + 1) * DH)
        qt = proj_ref[0, rows_q] * jnp.asarray(DH ** (-0.5), BF16)
        kt = proj_ref[0, width + head * DH : width + (head + 1) * DH]
        vt = proj_ref[0, 2 * width + head * DH : 2 * width + (head + 1) * DH]
        st = jnp.where(valid, tn(kt, qt), -1e30)
        top = jnp.max(st, axis=0, keepdims=True)
        et = jnp.exp(st - top)
        inverse = 1.0 / jnp.sum(et, axis=0, keepdims=True)
        low = et.astype(BF16)
        p_ref[0, head] = low
        inv_ref[0, head : head + 1] = inverse
        results.append(nn(vt, low) * inverse)
    obuf[step] = jnp.concatenate(results, axis=0).astype(BF16)

    def block_of(s, r):
        start = jnp.bitwise_xor(h, r) * part
        return obuf.at[s, :, pl.ds(pl.multiple_of(start, part), part)]

    def place_of(s, r):
        start = jnp.bitwise_xor(h, r) * width
        column = pl.ds(pl.multiple_of(s * part, part), part)
        return o_all.at[pl.ds(pl.multiple_of(start, width), width), column]

    def send_block(r, s):
        return remote(
            block_of(s, r), place_of(s, 0), send_o.at[r, s], recv_o.at[r, s], at(0, r)
        )

    def arrive_block(r, s):
        return remote(
            block_of(s, r), place_of(s, r), send_o.at[r, s], recv_o.at[r, s], at(0, r)
        )

    def keep_block(s):
        return pltpu.make_async_copy(block_of(s, 0), place_of(s, 0), keep_o.at[s])

    for r in (2, 3, 1):
        send_block(r, step).start()
    keep_block(step).start()

    slots(3)

    @pl.when(step == count - 1)
    def _():
        wt[3 * width :] = pt[0 : 3 * RANK]
        for j in range(3):
            part_j = slice(j * width, (j + 1) * width)
            delta = nn(up_t[part_j], pt[0 : 3 * RANK])
            wt[part_j] = (w_ref[j].astype(F32) + LOWRANK * delta).astype(BF16)
        to_head(1, later).wait_recv()
        pass_on(later).wait_recv()
        tile_a[...] = natural(1)
        per = owners // split
        for w in range(per):
            for k in range(split):
                blocks = [
                    entry(2, b * per + w)[:, 2 * RANK * k : 2 * RANK * (k + 1)]
                    for b in range(split)
                ]
                base = (w * split + k) * rows
                unpack[base : base + rows] = jnp.concatenate(blocks, axis=1)
        bt[...] = unpack[...].T.astype(BF16)
        finish(2, (3, 4))
        for c in range(len(chunks)):
            over_x(c).wait_send()
            for axis in (1, 2):
                spread_w(c, axis).wait_send()
                relay_w(c, axis).wait_send()
        for slot in (critical, later):
            for k in range(1, nd):
                to_dp(k, slot).wait_send()
            for b in (1, 2):
                to_head(b, slot).wait_send()
            pass_on(slot).wait_send()
        for s in range(count):
            keep_block(s).wait()
            for r in range(1, nh):
                send_block(r, s).wait_send()
                arrive_block(r, s).wait_recv()
        for w in range(3):
            sibling_own(w).wait()
            sibling_far(w).wait()


def attend(nd, nh, hidden, lengths, adapters_m, adapters_i, weight, bias, wo, wu, wd):
    count, keys, model = hidden.shape
    width = weight.shape[1]
    heads = width // DH
    tall = 3 * width + 3 * RANK
    part = keys // nh
    rows = adapters_m.shape[2]
    padded = -(-rows // 8) * 8
    shape = jax.ShapeDtypeStruct
    dma = pltpu.SemaphoreType.DMA
    return pl.pallas_call(
        functools.partial(attend_kernel, nd, nh),
        grid=(count,),
        in_specs=[
            pl.BlockSpec(memory_space=pltpu.SMEM),
            vmem(), vmem(), anywhere(), vmem(), vmem(), anywhere(), anywhere(), anywhere(),
        ],
        out_specs=[
            pl.BlockSpec((1, tall, keys), lambda s: (s, 0, 0)),
            pl.BlockSpec((1, heads, keys, keys), lambda s: (s, 0, 0, 0)),
            pl.BlockSpec((1, heads, keys), lambda s: (s, 0, 0)),
            anywhere(), anywhere(), anywhere(), anywhere(),
            vmem(), vmem(), vmem(), vmem(),
        ],
        out_shape=[
            shape((count, tall, keys), BF16),
            shape((count, heads, keys, keys), BF16),
            shape((count, heads, keys), F32),
            shape((nh * width, count * part), BF16),
            *[shape((nh - 1, *w.shape), BF16) for w in (wo, wu, wd)],
            shape((tall, model), BF16),
            shape((model, LANES), F32),
            shape((LANES, model), BF16),
            shape((LANES, width), BF16),
        ],
        scratch_shapes=[
            pltpu.VMEM((3, padded, LANES), F32),
            pltpu.VMEM((nh, nd, 1, padded, LANES), F32),
            pltpu.VMEM((nh, nd, 2, padded, LANES), F32),
            pltpu.VMEM((count, width, keys), BF16),
            pltpu.VMEM((model, 8), F32),
            pltpu.VMEM((model, LANES), F32),
            pltpu.VMEM((count, keys, model), BF16),
            pltpu.VMEM((count, 3 * width, keys), F32),
            pltpu.VMEM((3 * width, 3 * RANK), BF16),
            pltpu.VMEM((LANES, model), BF16),
            dma((count,)),
            dma((2, nd)), dma((2, nd)), dma((2, 4)), dma((2, 4)),
            dma((nh, count)), dma((nh, count)), dma((count,)),
            dma((5, 5)), dma((5, 5)), dma((2, 3)), dma((2, 3)),
        ],
        compiler_params=pltpu.CompilerParams(
            collective_id=1, has_side_effects=True, vmem_limit_bytes=VMEM_LIMIT
        ),
        name="attend",
    )(lengths, adapters_m, adapters_i, hidden, weight, bias, wo, wu, wd)


def tail_density(a):
    e = jnp.exp(-0.5 * a * a)
    t = 1.0 / (1.0 + (0.3275911 * 0.7071067811865476) * jnp.abs(a))
    poly = 1.061405429 * t - 1.453152027
    poly = poly * t + 1.421413741
    poly = poly * t - 0.284496736
    poly = poly * t + 0.254829592
    q = (0.5 * poly * t) * e
    return jnp.where(a >= 0, 1.0 - q, q), e * 0.3989422804014327


def centred(v):
    c = v - jnp.mean(v, axis=-1, keepdims=True)
    inverse = lax.rsqrt(jnp.mean(c * c, axis=-1, keepdims=True) + EPS_NORM)
    return c * inverse, inverse


def norm_back(e, n, inverse):
    return inverse * (
        e - jnp.mean(e, axis=-1, keepdims=True) - n * jnp.mean(e * n, axis=-1, keepdims=True)
    )


def token_kernel(
    nh, o_all, x_hbm, gout, wo_own, wo_rest, wu_own, wu_rest, wd_own, wd_rest,
    tile_a, bt, shifts, gains, up_bias,
    result, first, go, grads,
    x, wo, ocat, wu, wd, f, slope, h1, n1, i1, h1b, r2, gf, acc, gat, gbt, sem_x, sem_w,
):
    h = lax.axis_index("head")
    pairs, part, model = x.shape
    tokens = pairs * part
    width = wo_own.shape[0]
    relative = [jnp.bitwise_xor(h, r) for r in range(nh)]
    own = pltpu.make_async_copy(
        x_hbm.at[:, pl.ds(pl.multiple_of(h * part, part), part), :], x, sem_x
    )
    own.start()
    fetch = []
    for r in range(nh):
        a = wu_own if r == 0 else wu_rest.at[r - 1]
        b = wd_own if r == 0 else wd_rest.at[r - 1]
        fetch.append(
            (
                pltpu.make_async_copy(a, wu.at[r], sem_w.at[0, r]),
                pltpu.make_async_copy(b, wd.at[r], sem_w.at[1, r]),
            )
        )
    for r in range(nh):
        fetch[r][0].start()
    for r in range(nh):
        fetch[r][1].start()
    ocat[...] = o_all[...].T
    for r in range(nh):
        rows = pl.ds(pl.multiple_of(relative[r] * width, width), width)
        wo[rows] = wo_own[...] if r == 0 else wo_rest[r - 1]
    at = tile_a[...].T.astype(BF16)
    p3t, p4t, p8t, p9t = (at[m * RANK : (m + 1) * RANK] for m in range(4))
    p3 = tile_a[:, 0:RANK].astype(BF16)

    def inner(q, r):
        return bt[pl.ds(pl.multiple_of(relative[r] * 2 * RANK, 2 * RANK) + q * RANK, RANK), :]

    z_o = nt(ocat[...], p3t).astype(BF16)
    acc[...] = nn(ocat[...], wo[...]) + nn(z_o, p8t) * LOWRANK
    own.wait()
    v = x[...].reshape(tokens, model).astype(F32) + acc[...] + shifts[0:1]
    n, inv = centred(v)
    n1[...] = n
    i1[...] = inv
    h1[...] = n * gains[0:1] + shifts[1:2]
    h1b[...] = h1[...].astype(BF16)
    z_up = nt(h1b[...], p4t).astype(BF16)
    chunk = 256
    z_d = jnp.zeros((tokens, RANK), F32)
    for r in range(nh):
        fetch[r][0].wait()

        def up(c, carry, r=r):
            cols = pl.ds(pl.multiple_of(c * chunk, chunk), chunk)
            q1 = bt[
                pl.ds(pl.multiple_of(relative[r] * 2 * RANK, 2 * RANK) + RANK, RANK), cols
            ]
            a = (
                nn(h1b[...], wu[r, :, cols])
                + nn(z_up, q1) * LOWRANK
                + up_bias[pl.ds(relative[r], 1), cols]
            )
            cdf, density = tail_density(a)
            f[r, :, cols] = (a * cdf).astype(BF16)
            slope[r, :, cols] = (cdf + a * density).astype(BF16)
            return carry

        lax.fori_loop(0, model // chunk, up, 0)
        z_d = z_d + nt(f[r], inner(0, r))
    z_d = z_d.astype(BF16)
    for r in range(nh):
        fetch[r][1].wait()
        term = nn(f[r], wd[r])
        if r == 0:
            acc[...] = term + nn(z_d, p9t) * LOWRANK
        else:
            acc[...] += term
    n2, i2 = centred(h1[...] + acc[...] + shifts[2:3])
    result[...] = (n2 * gains[1:2] + shifts[3:4]).astype(BF16).reshape(result.shape)
    e = gout[...].reshape(tokens, model).astype(F32) * gains[1:2]
    r2[...] = norm_back(e, n2, i2)
    gf[...] = r2[...].astype(BF16)
    gzd = (nt(gf[...], p9t) * LOWRANK).astype(BF16)
    g9 = tn(z_d, gf[...]) * LOWRANK
    gzu = jnp.zeros((tokens, RANK), F32)
    for r in range(nh):
        gbt[pl.ds(pl.multiple_of(relative[r] * 2 * RANK, 2 * RANK), RANK), :] = tn(gzd, f[r])

        def down(c, carry, r=r):
            cols = pl.ds(pl.multiple_of(c * chunk, chunk), chunk)
            q0 = bt[pl.ds(pl.multiple_of(relative[r] * 2 * RANK, 2 * RANK), RANK), cols]
            df = nt(gf[...], wd[r, cols, :]) + nn(gzd, q0)
            slope[r, :, cols] = (df * slope[r, :, cols].astype(F32)).astype(BF16)
            return carry

        lax.fori_loop(0, model // chunk, down, 0)
        ga = slope[r]
        gzu = gzu + nt(ga, inner(1, r))
        gbt[pl.ds(pl.multiple_of(relative[r] * 2 * RANK, 2 * RANK) + RANK, RANK), :] = (
            tn(z_up, ga) * LOWRANK
        )
        term = nt(ga, wu[r])
        if r == 0:
            acc[...] = r2[...] + term
        else:
            acc[...] += term
    gzu = (gzu * LOWRANK).astype(BF16)
    g4 = tn(gzu, h1b[...])
    e = (acc[...] + nn(gzu, p4t)) * gains[0:1]
    r1 = norm_back(e, n1[...], i1[...])
    first[...] = r1.reshape(first.shape)
    gat[...] = r1.astype(BF16)
    gzo = (nt(gat[...], p8t) * LOWRANK).astype(BF16)
    g8 = tn(z_o, gat[...]) * LOWRANK
    g3 = tn(gzo, ocat[...])
    go[...] = (nt(wo[...], gat[...]) + nt(p3, gzo)).astype(BF16)
    zeros = jnp.zeros((4 * RANK, model), F32)
    grads[0] = jnp.concatenate([g3, g4, g8, g9, zeros], axis=0).T
    grads[1] = gbt[...].T


def token_side(o_all, hidden, gout, wo, wu, wd, tile_a, bt, shifts, gains, up_bias):
    pairs, part, model = gout.shape
    tokens = pairs * part
    width = wo[0].shape[0]
    nh = model // width
    shape = jax.ShapeDtypeStruct
    return pl.pallas_call(
        functools.partial(token_kernel, nh),
        out_shape=[
            shape((pairs, part, model), BF16),
            shape((pairs, part, model), F32),
            shape((model, tokens), BF16),
            shape((2, model, LANES), F32),
        ],
        in_specs=[vmem(), anywhere(), vmem(), vmem(), vmem()] + [anywhere()] * 4 + [vmem()] * 5,
        out_specs=[vmem()] * 4,
        scratch_shapes=[
            pltpu.VMEM((pairs, part, model), BF16),
            pltpu.VMEM((model, model), BF16),
            pltpu.VMEM((tokens, model), BF16),
            pltpu.VMEM((nh, model, model), BF16),
            pltpu.VMEM((nh, model, model), BF16),
            pltpu.VMEM((nh, tokens, model), BF16),
            pltpu.VMEM((nh, tokens, model), BF16),
            pltpu.VMEM((tokens, model), F32),
            pltpu.VMEM((tokens, model), F32),
            pltpu.VMEM((tokens, 1), F32),
            pltpu.VMEM((tokens, model), BF16),
            pltpu.VMEM((tokens, model), F32),
            pltpu.VMEM((tokens, model), BF16),
            pltpu.VMEM((tokens, model), F32),
            pltpu.VMEM((tokens, model), BF16),
            pltpu.VMEM((LANES, model), F32),
            pltpu.SemaphoreType.DMA,
            pltpu.SemaphoreType.DMA((2, nh)),
        ],
        compiler_params=pltpu.CompilerParams(vmem_limit_bytes=VMEM_LIMIT),
        name="token_side",
    )(o_all, hidden, gout, *wo, *wu, *wd, tile_a, bt, shifts, gains, up_bias)


def attend_back_kernel(
    nd, nh, x_ref, proj_ref, p_ref, inv_ref, go, first, early, wt, down_t,
    roots_m, roots_i, roots_r,
    grad_in, gradients, step_m, step_i, squares,
    got_all, gproj, grad_t, late, whole_buf, near, far, last, blocks, mixed, sq, sq_head, sq_dp,
    send_g, recv_g, keep_g, send_n, recv_n, send_f, recv_f,
    send_a, recv_a, send_b, recv_b, *rest,
):
    step = pl.program_id(0)
    d, h = lax.axis_index("dp"), lax.axis_index("head")
    relative = [jnp.bitwise_xor(h, r) for r in range(nh)]
    count, part, model = first.shape
    width = got_all.shape[1]
    own_rows = pl.ds(pl.multiple_of(h * width, width), width)
    one = Reduction(nd, nh, rest[0:4], rest[8:14])
    two = Reduction(nd, nh, rest[4:8], rest[14:20])

    def at(b):
        return (d, jnp.bitwise_xor(h, b))

    def block_of(r, s):
        return go.at[
            pl.ds(pl.multiple_of(relative[r] * width, width), width),
            pl.ds(pl.multiple_of(s * part, part), part),
        ]

    def place_of(r, s):
        return got_all.at[s, :, pl.ds(pl.multiple_of(relative[r] * part, part), part)]

    def bring(r, s):
        return remote(
            block_of(r, s), place_of(0, s), send_g.at[r, s], recv_g.at[r, s], at(r)
        )

    def brought(r, s):
        return remote(
            block_of(r, s), place_of(r, s), send_g.at[r, s], recv_g.at[r, s], at(r)
        )

    def keep(s):
        return pltpu.make_async_copy(block_of(0, s), place_of(0, s), keep_g.at[s])

    def to_near(i, s):
        return remote(
            whole_buf.at[s, relative[1 + 2 * i]], near.at[s, i], send_n.at[i, s],
            recv_n.at[i, s], at(1),
        )

    def to_far(s):
        return remote(far.at[s], last.at[s], send_f.at[s], recv_f.at[s], at(2))

    def pass_far(s):
        to_near(1, s).wait_recv()
        far[s] = (whole_buf[s, relative[2]].astype(F32) + near[s, 1].astype(F32)).astype(BF16)
        to_far(s).start()

    def complete(s):
        to_near(0, s).wait_recv()
        to_far(s).wait_recv()
        grad_in[s] = (
            first[s]
            + whole_buf[s, h].astype(F32)
            + near[s, 0].astype(F32)
            + last[s].astype(F32)
        ).astype(BF16)

    @pl.when(step == 0)
    def _():
        greet_signal(nd, nh)
        for s in range(count):
            keep(s).start()
        grad_t[...] = jnp.zeros_like(grad_t)
        greet_wait(nd, nh)
        for s in range(count):
            for r in (2, 3, 1):
                bring(r, s).start()
        two.start(early[...])

    keep(step).wait()
    for r in range(1, nh):
        brought(r, step).wait_recv()
    got = got_all.at[step]
    scale = jnp.asarray(DH ** (-0.5), BF16)
    for head in range(width // DH):
        part_h = slice(head * DH, (head + 1) * DH)
        rows_k = slice(width + head * DH, width + (head + 1) * DH)
        rows_v = slice(2 * width + head * DH, 2 * width + (head + 1) * DH)
        inverse = inv_ref[0, head : head + 1]
        qt = proj_ref[0, part_h] * scale
        kt = proj_ref[0, rows_k] * scale
        vt = proj_ref[0, rows_v]
        gs = (got[part_h].astype(F32) * inverse).astype(BF16)
        et = p_ref[0, head]
        ef = et.astype(F32)
        dpt = tn(vt, gs)
        delta = jnp.sum(ef * dpt, axis=0, keepdims=True) * inverse
        gst = (ef * (dpt - delta)).astype(BF16)
        gproj[part_h] = nn(kt, gst).astype(BF16)
        gproj[rows_k] = nt(qt, gst).astype(BF16)
        gproj[rows_v] = nt(gs, et).astype(BF16)
        if head == 1:

            @pl.when(step >= 1)
            def _():
                pass_far(jnp.maximum(step - 1, 0))

    inner = []
    for j in range(3):
        block = gproj[j * width : (j + 1) * width]
        ut = proj_ref[0, 3 * width + j * RANK : 3 * width + (j + 1) * RANK]
        grad_t[(3 + j) * RANK : (4 + j) * RANK, 0:width] += nt(ut, block) * LOWRANK
        inner.append(nn(down_t[(3 + j) * RANK : (4 + j) * RANK], block) * LOWRANK)
    inner = jnp.concatenate(inner, axis=0).astype(BF16)
    grad_t[0 : 3 * RANK] += nn(inner, x_ref[0])
    whole_buf[step] = tn(gproj[...], wt[0 : 3 * width]).astype(BF16).reshape(nh, part, model)
    to_near(1, step).start()
    to_near(0, step).start()

    @pl.when(step == 1)
    def _():
        two.over_dp()

    @pl.when(step == 2)
    def _():
        two.over_head(0)

    @pl.when(step == 3)
    def _():
        two.over_head(1)

    def preconditioned(j, u, where, i):
        where[i] = u
        sq[j : j + 1] = jnp.broadcast_to(
            jnp.sum(jnp.sum(u * u, axis=0, keepdims=True), axis=1, keepdims=True), (1, LANES)
        )

    def mix(t):
        mixed[t] = tn(blocks[t], gradients[t].T, HIGH).astype(BF16)

    def steps_model(t):
        for j in range(roots_m.shape[0]):
            tile, m = slot_of(j)
            if tile == t:
                g = mixed[t, m * RANK : (m + 1) * RANK]
                preconditioned(j, nt(g, roots_m[j].astype(BF16)), step_m, j)

    @pl.when(step == count - 1)
    def _():
        full = grad_t[...].T
        lane = lax.broadcasted_iota(jnp.int32, full.shape, 1)
        late[0] = jnp.where(lane < 3 * RANK, full, 0.0)
        rows = full[0:width]
        lane = lax.broadcasted_iota(jnp.int32, rows.shape, 1)
        late[0, own_rows, :] = jnp.where(lane < 3 * RANK, late[0, own_rows, :], rows)
        one.start(late[...])
        pass_far(count - 1)
        blocks[...] = jnp.zeros_like(blocks)
        sq[...] = jnp.zeros_like(sq)
        for j in range(roots_m.shape[0]):
            t, m = slot_of(j)
            blocks[t, m * RANK : (m + 1) * RANK, m * RANK : (m + 1) * RANK] = roots_r[j]
        split = roots_i.shape[2] // model
        for k in range(split):
            for q in range(2):
                m = 2 * k + q
                blocks[2, m * RANK : (m + 1) * RANK, m * RANK : (m + 1) * RANK] = roots_r[
                    roots_m.shape[0] + q
                ]
        two.finish(gradients.at[1:3])
        one.over_dp()
        mix(1)
        mix(2)
        for q in range(2):
            u = jnp.zeros((RANK, roots_i.shape[1]), F32)
            for k in range(split):
                m = 2 * k + q
                u = u + nt(
                    mixed[2, m * RANK : (m + 1) * RANK],
                    roots_i[q, :, k * model : (k + 1) * model].astype(BF16),
                )
            preconditioned(roots_m.shape[0] + q, u, step_i, q)
        one.over_head(0)
        steps_model(1)
        one.over_head(1)
        for s in range(count):
            complete(s)
        one.finish(gradients.at[0:1])
        mix(0)
        steps_model(0)

        def sq_over_head(k):
            return remote(
                sq, sq_head.at[k], send_a.at[k], recv_a.at[k], (d, lax.rem(h + k, nh))
            )

        def sq_over_dp(k):
            return remote(
                sq_dp.at[0], sq_dp.at[k], send_b.at[k], recv_b.at[k], (lax.rem(d + k, nd), h)
            )

        for k in range(1, nh):
            sq_over_head(k).start()
        total = sq[...]
        for k in range(1, nh):
            sq_over_head(k).wait_recv()
            total = total + sq_head[k]
        sq_dp[0] = total
        for k in range(1, nd):
            sq_over_dp(k).start()
        for k in range(1, nd):
            sq_over_dp(k).wait_recv()
            total = total + sq_dp[k]
        squares[...] = total
        for k in range(1, nh):
            sq_over_head(k).wait_send()
        for k in range(1, nd):
            sq_over_dp(k).wait_send()
        for s in range(count):
            to_far(s).wait_send()
            for i in range(2):
                to_near(i, s).wait_send()
            for r in range(1, nh):
                bring(r, s).wait_send()


def attend_back(
    nd, nh, hidden, proj, p, inverse, go, first, early, wt, down_t, roots_m, roots_i, roots_r
):
    count, keys, model = hidden.shape
    part, width = first.shape[1], model // nh
    heads = width // DH
    tall = 3 * width + 3 * RANK
    shape = jax.ShapeDtypeStruct
    dma = pltpu.SemaphoreType.DMA
    bufs_one, sems_one = Reduction.scratch(nd, nh, 1, model)
    bufs_two, sems_two = Reduction.scratch(nd, nh, 2, model)
    return pl.pallas_call(
        functools.partial(attend_back_kernel, nd, nh),
        grid=(count,),
        in_specs=[
            pl.BlockSpec((1, keys, model), lambda s: (s, 0, 0)),
            pl.BlockSpec((1, tall, keys), lambda s: (s, 0, 0)),
            pl.BlockSpec((1, heads, keys, keys), lambda s: (s, 0, 0, 0)),
            pl.BlockSpec((1, heads, keys), lambda s: (s, 0, 0)),
            anywhere(),
            *[vmem()] * 7,
        ],
        out_specs=[vmem()] * 5,
        out_shape=[
            shape((count, part, model), BF16),
            shape((3, model, LANES), F32),
            shape((roots_m.shape[0], RANK, roots_m.shape[1]), F32),
            shape((2, RANK, roots_i.shape[1]), F32),
            shape((16, LANES), F32),
        ],
        scratch_shapes=[
            pltpu.VMEM((count, width, keys), BF16),
            pltpu.VMEM((3 * width, keys), BF16),
            pltpu.VMEM((LANES, model), F32),
            pltpu.VMEM((1, model, LANES), F32),
            pltpu.VMEM((count, nh, part, model), BF16),
            pltpu.VMEM((count, 2, part, model), BF16),
            pltpu.VMEM((count, part, model), BF16),
            pltpu.VMEM((count, part, model), BF16),
            pltpu.VMEM((3, LANES, LANES), F32),
            pltpu.VMEM((3, LANES, model), BF16),
            pltpu.VMEM((16, LANES), F32),
            pltpu.VMEM((nh, 16, LANES), F32),
            pltpu.VMEM((nd, 16, LANES), F32),
            dma((nh, count)), dma((nh, count)), dma((count,)),
            dma((2, count)), dma((2, count)), dma((count,)), dma((count,)),
            dma((nh,)), dma((nh,)), dma((nd,)), dma((nd,)),
            *bufs_one, *bufs_two, *sems_one, *sems_two,
        ],
        compiler_params=pltpu.CompilerParams(
            collective_id=2, has_side_effects=True, vmem_limit_bytes=VMEM_LIMIT
        ),
        name="attend_back",
    )(hidden, proj, p, inverse, go, first, early, wt, down_t, roots_m, roots_i, roots_r)


def finish_kernel(
    nh, owners, grad_in, g_ref, stats_m, stats_i, stats_r, am, ai, step_m, step_i, squares,
    grad_out, grad_m, grad_i, adapt_m, adapt_i, new_m, new_i, new_r, gt,
):
    grad_out[...] = grad_in[...]
    owner = lax.axis_index("dp") * nh + lax.axis_index("head")
    count, rows, model = stats_m.shape
    rows_i = stats_i.shape[1]
    for t in range(3):
        gt[t] = g_ref[t].T.astype(BF16)
    own = [g_ref[t, pl.ds(owner * rows, rows), :] for t in range(2)]
    turned = [v.T for v in own]

    def update(j, old, u, rate):
        size = model if j < count else rows_i * owners
        mean = squares[j : j + 1, 0:1] * (1.0 / (size * RANK))
        return old - rate * lax.rsqrt(mean + 1e-6) * u

    for j in range(count):
        t, m = slot_of(j)
        lanes = slice(m * RANK, (m + 1) * RANK)
        full = gt[t, lanes]
        grad_m[j] = turned[t][lanes]
        new_m[j] = DECAY * stats_m[j] + (1.0 - DECAY) * nn(own[t][:, lanes].astype(BF16), full)
        new_r[j] = DECAY * stats_r[j] + (1.0 - DECAY) * nt(full, full)
        adapt_m[j] = update(j, am[j], step_m[j], RATE_FIRST if j < 5 else RATE_SECOND)
    blocks = stats_i.shape[2] // model
    per = model // rows_i
    block = owner // per
    tall = g_ref[2, pl.ds((owner - block * per) * rows_i, rows_i), :]
    tall_t = tall.T
    for q in range(2):
        mine = jnp.zeros((rows_i, RANK), F32)
        mine_t = jnp.zeros((RANK, rows_i), F32)
        gram = jnp.zeros((RANK, RANK), F32)
        for k in range(blocks):
            lanes = slice((2 * k + q) * RANK, (2 * k + q + 1) * RANK)
            mine = jnp.where(block == k, tall[:, lanes], mine)
            mine_t = jnp.where(block == k, tall_t[lanes], mine_t)
        grad_i[q] = mine_t
        mine = mine.astype(BF16)
        for k in range(blocks):
            lanes = slice((2 * k + q) * RANK, (2 * k + q + 1) * RANK)
            cols = slice(k * model, (k + 1) * model)
            full = gt[2, lanes]
            gram = gram + nt(full, full)
            new_i[q, :, cols] = DECAY * stats_i[q, :, cols] + (1.0 - DECAY) * nn(mine, full)
        new_r[count + q] = DECAY * stats_r[count + q] + (1.0 - DECAY) * gram
        adapt_i[q] = update(count + q, ai[q], step_i[q], RATE_FIRST if q < 1 else RATE_SECOND)


def finish(nd, nh, grad_in, g, stats_m, stats_i, stats_r, am, ai, step_m, step_i, squares):
    shape = jax.ShapeDtypeStruct
    model = stats_m.shape[2]
    return pl.pallas_call(
        functools.partial(finish_kernel, nh, nd * nh),
        in_specs=[vmem()] * 10,
        out_specs=[vmem()] * 8,
        out_shape=[
            shape(grad_in.shape, BF16),
            shape(am.shape, F32),
            shape(ai.shape, F32),
            shape(am.shape, F32),
            shape(ai.shape, F32),
            shape(stats_m.shape, F32),
            shape(stats_i.shape, F32),
            shape(stats_r.shape, F32),
        ],
        scratch_shapes=[pltpu.VMEM((3, LANES, model), BF16)],
        compiler_params=pltpu.CompilerParams(vmem_limit_bytes=VMEM_LIMIT),
        name="finish",
    )(grad_in, g, stats_m, stats_i, stats_r, am, ai, step_m, step_i, squares)


def local(
    nd,
    nh,
    hidden_input,
    grad_out,
    pair_lengths,
    query_key_value_weight,
    qkv_bias,
    output_projection_weight,
    shifts,
    gains,
    up_projection_weight,
    up_bias,
    down_projection_weight,
    adapters_model,
    adapters_inner,
    stats_model,
    stats_inner,
    stats_rank,
    roots_model,
    roots_inner,
    roots_rank,
):
    model = hidden_input.shape[2]
    turned_m = jnp.swapaxes(adapters_model, 1, 2)
    turned_i = jnp.swapaxes(adapters_inner, 1, 2)
    proj, p, inverse, o_all, wo_rest, wu_rest, wd_rest, wt, tile_a, bt, down_t = attend(
        nd, nh, hidden_input, pair_lengths, turned_m, turned_i,
        jnp.swapaxes(query_key_value_weight, 1, 2), qkv_bias,
        output_projection_weight, up_projection_weight, down_projection_weight,
    )
    result, first, go, early = token_side(
        o_all, hidden_input, grad_out,
        (output_projection_weight, wo_rest), (up_projection_weight, wu_rest),
        (down_projection_weight, wd_rest), tile_a, bt, shifts, gains, up_bias.reshape(nh, model),
    )
    grad_in, gradients, step_m, step_i, squares = attend_back(
        nd, nh, hidden_input, proj, p, inverse, go, first, early, wt, down_t,
        roots_model, roots_inner, roots_rank,
    )
    grad_in, grad_m, grad_i, adapt_m, adapt_i, new_m, new_i, new_r = finish(
        nd, nh, grad_in, gradients, stats_model, stats_inner, stats_rank, turned_m, turned_i,
        step_m, step_i, squares,
    )
    grad_m, grad_i, adapt_m, adapt_i = (
        jnp.swapaxes(v, 1, 2) for v in (grad_m, grad_i, adapt_m, adapt_i)
    )
    return (result, grad_in, grad_m, grad_i, adapt_m, adapt_i, new_m, new_i, new_r)


def solution(mesh):
    rows = P(None, ("dp", "head"), None)
    in_specs = (
        P("dp", None, None),
        P("dp", "head", None),
        P("dp"),
        P(None, None, "head"),
        P(),
        P("head", None),
        P(),
        P(),
        P(None, "head"),
        P(),
        P("head", None),
        rows, rows, rows, rows,
        P(),
        rows, rows,
        P(),
    )
    out_specs = (
        P("dp", "head", None),
        P("dp", "head", None),
        rows, rows, rows, rows, rows, rows,
        P(),
    )
    body = functools.partial(local, mesh.shape["dp"], mesh.shape["head"])
    return jax.shard_map(body, mesh=mesh, in_specs=in_specs, out_specs=out_specs, check_vma=False)
```

profile of v0, /device:TPU:0, one launch (start us, length us, event | category | flops | bytes accessed | tf_op | source)
XLA Modules:
  0.0 165.7 jit_solution(11782017853829859141)
XLA Ops:
  0.6 1.3 reshape.21.up_bias
  2.0 50.8 %attend.1 = (bf16[5,624,512]{2,1,0:T(8,128)(2,1)}, bf16[5,3,512,512]{3,2,1,0:T(8,128)(2,1)}, f32[5,3,512]{2,1,0:T(4,128)}, bf16[768,640]{1,0:T(8,128)(2,1)}, bf1...) custom-call(s32[5]{0:T(128)} %lengths.1, ...), custom_call_target="tpu_custom_call" | custom-call | tf_op jit(solution)/shard_map/attend/pallas_call | solution.py:478
  52.7 43.9 %token_side.1 = (bf16[5,128,768]{2,1,0:T(8,128)(2,1)}, f32[5,128,768]{2,1,0:T(8,128)}, bf16[768,640]{1,0:T(8,128)(2,1)}, f32[2,768,128]{2,1,0:T(8,128)}) custom-call(bf16[768,640]{1,0:T(8,128)(2,1)} %get-tuple-element.37.o_all, bf16[5,512,768]{2,1,0:T(8,128)(2,1)} %x_ref.1, bf16[5,128,768]{2,1,0:T(8,128)(2,1)} %gout.1, bf16[192,768]{1,0:T(8,128)(2,1)} %wo_own.1, ...), custom_call_target="tpu_custom_call" | custom-call | tf_op jit(solution)/shard_map/token_side/pallas_call | solution.py:679
  96.6 63.7 %attend_back.1 = (bf16[5,128,768]{2,1,0:T(8,128)(2,1)}, f32[3,768,128]{2,1,0:T(8,128)}, f32[10,16,24]{2,1,0:T(8,128)}, f32[2,16,96]{2,1,0:T(8,128)}, f32[16,128]{1,0:T(8,128)}) custom-call(bf16[5,512,768]{2,1,0:T(8,128)(2,1)} %x_ref.1, bf16[5,624,512]{2,1,0:T(8,128)(2,1)} %get-tuple-element.44.proj_ref, bf16[5,3,512,512]{3,2,1,0:T(8,128)(2,1)} %get-tuple-element.45.p_ref, ...), custom_call_target="tpu_custom_call" | custom-call | tf_op jit(solution)/shard_map/attend_back/pallas_call | solution.py:950
  160.3 5.4 %finish.1 = (bf16[5,128,768]{2,1,0:T(8,128)(2,1)}, f32[10,16,24]{2,1,0:T(8,128)}, f32[2,16,96]{2,1,0:T(8,128)}, f32[10,16,24]{2,1,0:T(8,128)}, f32[2,16,96]{2,1,...) custom-call(bf16[5,128,768]{2,1,0:T(8,128)(2,1)} %get-tuple-element.52.grad_in, ...), custom_call_target="tpu_custom_call" | custom-call | tf_op jit(solution)/shard_map/finish/pallas_call | solution.py:1049
where the time goes:
time: 166 us
  Pallas kernels  164 us (99%)
    pallas_call x1, Pallas kernels, attend_back(): pl.pallas_call(functools.partial(attend_back_kernel, nd, nh), grid=(count...  63.7 us
    pallas_call x1, Pallas kernels, attend(): pl.pallas_call(functools.partial(attend_kernel, nd, nh), grid=(count,), i...  50.8 us
    pallas_call x1, Pallas kernels, token_side(): pl.pallas_call(functools.partial(token_kernel, nh), out_shape=[shape((pai...  43.9 us
    pallas_call x1, Pallas kernels, finish(): pl.pallas_call(functools.partial(finish_kernel, nh, nd * nh), in_specs=[v...  5.37 us

commit v1 on v0

--- a/solution.py
+++ b/solution.py
@@ -165,34 +165,64 @@
             self.across(i).wait_send()
 
 
-def attend_kernel(
-    nd, nh, lengths, am, ai, x_hbm, w_ref, bias_ref, wo, wu, wd,
-    proj_ref, p_ref, inv_ref, o_all, go_w, gu_w, gd_w, wt, tile_a, bt, down_t,
-    packed, first_tile, other_tiles, obuf, bias_col, unpack, x_ref, raw, up_t, pt,
-    load_x,
+def cdf_and_density(a):
+    cdf = 0.5 * (1.0 + lax.erf(a * 0.7071067811865476))
+    return cdf, jnp.exp(-0.5 * a * a) * 0.3989422804014327
+
+
+def centred(v):
+    c = v - jnp.mean(v, axis=-1, keepdims=True)
+    inverse = lax.rsqrt(jnp.mean(c * c, axis=-1, keepdims=True) + EPS_NORM)
+    return c * inverse, inverse
+
+
+def norm_back(e, n, inverse):
+    return inverse * (
+        e - jnp.mean(e, axis=-1, keepdims=True) - n * jnp.mean(e * n, axis=-1, keepdims=True)
+    )
+
+
+def forward_kernel(
+    nd, nh, lengths, am, ai, x_ref, x_hbm, w_ref, bias_ref, wo_own, wu_own, wd_own,
+    gout, shifts, gains, up_bias,
+    proj_ref, p_ref, inv_ref, wt, down_t, result_out, gat_out, go_out, grads_out,
+    packed, first_tile, other_tiles, obuf, bias_col, unpack, tile_a, bt,
+    o_all, wo, wu, wd, x, ocat, f, slope, h1, n1, i1, h1b, r2, gf, acc, gat, gbt, result, go, grads,
     send_d, recv_d, send_h, recv_h, send_o, recv_o, keep_o, send_w, recv_w, send_s, recv_s,
+    load, store,
 ):
     step = pl.program_id(0)
+    last = pl.num_programs(0) - 1
     d, h = lax.axis_index("dp"), lax.axis_index("head")
-    count, keys, model = x_ref.shape
-    part = keys // nh
+    count, part, model = x.shape
+    tokens = count * part
     width = w_ref.shape[1]
+    keys = x_ref.shape[1]
     rows = am.shape[2]
     split = ai.shape[2] // rows
     owners = nd * nh
     quarter = lax.rem(d, 4)
+    relative = [jnp.bitwise_xor(h, r) for r in range(nh)]
 
     def at(a, b):
         return (jnp.bitwise_xor(d, a), jnp.bitwise_xor(h, b))
 
-    own_w = (wo, wu, wd)
-    all_w = (go_w, gu_w, gd_w)
+    def window(start, size):
+        return pl.ds(pl.multiple_of(start * size, size), size)
+
+    own_w = (wo_own, wu_own, wd_own)
+
+    def piece(w, source, slot):
+        if w == 0:
+            return wo.at[window(relative[source], width)]
+        return (wu, wd)[w - 1].at[slot]
+
     chunks = []
     for w in range(3):
         quarter_rows = own_w[w].shape[0] // 4
         pieces = 1 if w == 0 else 2
-        for piece in range(pieces):
-            chunks.append((w, quarter_rows, piece * quarter_rows // pieces, quarter_rows // pieces))
+        for n in range(pieces):
+            chunks.append((w, quarter_rows, n * quarter_rows // pieces, quarter_rows // pieces))
 
     def region(ref, c, who, half=None):
         w, quarter_rows, offset, size = chunks[c]
@@ -205,28 +235,40 @@
     def over_x(c):
         w = chunks[c][0]
         return remote(
-            region(own_w[w], c, 0), region(all_w[w].at[1], c, 0),
+            region(own_w[w], c, 0), region(piece(w, 0, 2), c, 0),
             send_w.at[0, c], recv_w.at[0, c], at(0, 2),
         )
 
+    def over_x_here(c):
+        w = chunks[c][0]
+        return remote(
+            region(own_w[w], c, 0), region(piece(w, 2, 2), c, 0),
+            send_w.at[0, c], recv_w.at[0, c], at(0, 2),
+        )
+
     def spread_w(c, axis):
-        here = region(all_w[chunks[c][0]].at[1], c, 0)
+        here = region(piece(chunks[c][0], 2, 2), c, 0)
         return remote(here, here, send_w.at[axis, c], recv_w.at[axis, c], at(axis, 0))
 
     def relay_w(c, axis):
-        here = region(all_w[chunks[c][0]].at[1], c, 3 - axis, axis - 1)
+        here = region(piece(chunks[c][0], 2, 2), c, 3 - axis, axis - 1)
         return remote(here, here, send_w.at[2 + axis, c], recv_w.at[2 + axis, c], at(axis, 0))
 
     def sibling_own(w):
-        return remote(own_w[w], all_w[w].at[0], send_s.at[0, w], recv_s.at[0, w], at(0, 1))
+        return remote(
+            own_w[w], piece(w, 0, 1), send_s.at[0, w], recv_s.at[0, w], at(0, 1)
+        )
 
     def sibling_far(w):
         return remote(
-            all_w[w].at[1], all_w[w].at[2], send_s.at[1, w], recv_s.at[1, w], at(0, 1)
-        )
+            piece(w, 2, 2), piece(w, 2, 3), send_s.at[1, w], recv_s.at[1, w], at(0, 1)
+        )
+
+    def keep_w(w):
+        return pltpu.make_async_copy(own_w[w], piece(w, 0, 0), load.at[w])
 
     def forward(c):
-        over_x(c).wait_recv()
+        over_x_here(c).wait_recv()
         spread_w(c, 2).start()
         spread_w(c, 1).start()
 
@@ -236,13 +278,10 @@
         spread_w(c, 1).wait_recv()
         relay_w(c, 2).start()
 
-    def arrived(c):
-        relay_w(c, 1).wait_recv()
-        relay_w(c, 2).wait_recv()
-
     def finish(w, which):
         for c in which:
-            arrived(c)
+            relay_w(c, 1).wait_recv()
+            relay_w(c, 2).wait_recv()
         sibling_far(w).start()
 
     stores = (first_tile, other_tiles)
@@ -271,18 +310,21 @@
     def natural(t):
         return jnp.concatenate([entry(t, i) for i in range(owners)], axis=0)
 
-    def fetch_x(i):
-        return pltpu.make_async_copy(x_hbm.at[i], x_ref.at[i], load_x.at[i])
-
-    def project(i):
-        fetch_x(i).wait()
-        for j in range(3):
-            raw[i, j * width : (j + 1) * width] = nt(w_ref[j], x_ref[i])
+    def later_to_head():
+        for k in range(1, nd):
+            to_dp(k, later).wait_recv()
+        to_head(2, later).start()
+        to_head(1, later).start()
+
+    def later_pass_on():
+        to_head(2, later).wait_recv()
+        pass_on(later).start()
+
+    def own_rows():
+        return pltpu.make_async_copy(x_hbm.at[:, window(h, part), :], x, load.at[3])
 
     @pl.when(step == 0)
     def _():
-        for i in range(count):
-            fetch_x(i).start()
         greet_signal(nd, nh)
         packed[...] = jnp.zeros_like(packed)
         groups = [
@@ -297,73 +339,51 @@
             packed[t, 0:rows] = jnp.concatenate(group, axis=0).T.astype(BF16).astype(F32)
         first_tile[h, d] = packed[0:1]
         other_tiles[h, d] = packed[1:3]
-        project(0)
         greet_wait(nd, nh)
         for k in range(1, nd):
             to_dp(k, critical).start()
         over_x(0).start()
         over_x(1).start()
-        project(1)
-        project(2)
+        bias_col[...] = jnp.concatenate(
+            [bias_ref[...], jnp.zeros((5, model), F32)], axis=0
+        ).T
         for k in range(1, nd):
             to_dp(k, critical).wait_recv()
         to_head(2, critical).start()
         to_head(1, critical).start()
         for c in range(2, len(chunks)):
             over_x(c).start()
-        project(3)
+        for w in range(3):
+            sibling_own(w).start()
+            keep_w(w).start()
+        own_rows().start()
         to_head(2, critical).wait_recv()
         pass_on(critical).start()
-        sibling_own(0).start()
-        sibling_own(1).start()
-        sibling_own(2).start()
-        project(4)
-        bias_col[...] = jnp.concatenate(
-            [bias_ref[...], jnp.zeros((5, model), F32)], axis=0
-        ).T
         to_head(1, critical).wait_recv()
         pass_on(critical).wait_recv()
         pn = natural(0)
-        pt[...] = pn.T.astype(BF16)
+        pt = pn.T.astype(BF16)
         tile_a[...] = pn
-        own = tile_a[pl.ds(pl.multiple_of(h * width, width), width), :]
+        own = tile_a[window(h, width), :]
         down_t[...] = own.T.astype(BF16)
-        own = own[:, 3 * RANK : 6 * RANK].astype(BF16)
-        lane = lax.broadcasted_iota(jnp.int32, own.shape, 1)
+        own = own.astype(BF16)
+        wt[3 * width :] = pt[0 : 3 * RANK]
         for j in range(3):
-            inside = (lane >= j * RANK) & (lane < (j + 1) * RANK)
-            up_t[j * width : (j + 1) * width] = jnp.where(inside, own, jnp.zeros_like(own))
+            delta = nn(own[:, (3 + j) * RANK : (4 + j) * RANK], pt[j * RANK : (j + 1) * RANK])
+            wt[j * width : (j + 1) * width] = (w_ref[j].astype(F32) + LOWRANK * delta).astype(
+                BF16
+            )
         for k in range(1, nd):
             to_dp(k, later).start()
 
-    inner = nt(pt[0 : 3 * RANK], x_ref[step]).astype(BF16)
-    proj_ref[0, 3 * width :] = inner
-    mine = pl.ds(pl.multiple_of(h * width, width), width)
+    proj = nt(wt[...], x_ref[0])
+    mine = window(h, width)
     for j in range(3):
-        part_j = slice(j * width, (j + 1) * width)
-        proj_ref[0, part_j] = (
-            raw[step, part_j] + LOWRANK * nn(up_t[part_j], inner) + bias_col[mine, j : j + 1]
+        proj_ref[0, j * width : (j + 1) * width] = (
+            proj[j * width : (j + 1) * width] + bias_col[mine, j : j + 1]
         ).astype(BF16)
+    proj_ref[0, 3 * width :] = proj[3 * width :].astype(BF16)
     valid = lax.broadcasted_iota(jnp.int32, (keys, 1), 0) < lengths[step]
-
-    def slot(s, place):
-        for action in plan.get((s, place), ()):
-            action()
-
-    def slots(place):
-        for s in range(count):
-            if (s, place) in plan:
-                pl.when(step == s)(functools.partial(slot, s, place))
-
-    def later_to_head():
-        for k in range(1, nd):
-            to_dp(k, later).wait_recv()
-        to_head(2, later).start()
-        to_head(1, later).start()
-
-    def later_pass_on():
-        to_head(2, later).wait_recv()
-        pass_on(later).start()
 
     bind = functools.partial
     plan = {
@@ -371,12 +391,21 @@
         (0, 1): [bind(forward, 1)],
         (1, 1): [bind(forward, 2), bind(relay, 0)],
         (1, 3): [later_to_head, bind(relay, 1)],
-        (2, 1): [bind(forward, 3)],
-        (2, 3): [bind(forward, 4), bind(relay, 2)],
-        (3, 1): [bind(relay, 3), bind(finish, 0, (0,))],
-        (3, 3): [later_pass_on, bind(relay, 4)],
-        (4, 1): [bind(finish, 1, (1, 2))],
+        (2, 1): [bind(finish, 0, (0,))],
+        (2, 3): [bind(forward, 3), bind(relay, 2)],
+        (3, 1): [later_pass_on],
+        (3, 3): [bind(finish, 1, (1, 2)), bind(forward, 4)],
+        (4, 1): [bind(relay, 3)],
     }
+
+    def slots(place):
+        for s in range(count):
+            if (s, place) in plan:
+
+                @pl.when(step == s)
+                def _(s=s):
+                    for action in plan[s, place]:
+                        action()
 
     results = []
     for head in range(width // DH):
@@ -396,13 +425,10 @@
     obuf[step] = jnp.concatenate(results, axis=0).astype(BF16)
 
     def block_of(s, r):
-        start = jnp.bitwise_xor(h, r) * part
-        return obuf.at[s, :, pl.ds(pl.multiple_of(start, part), part)]
+        return obuf.at[s, :, window(relative[r], part)]
 
     def place_of(s, r):
-        start = jnp.bitwise_xor(h, r) * width
-        column = pl.ds(pl.multiple_of(s * part, part), part)
-        return o_all.at[pl.ds(pl.multiple_of(start, width), width), column]
+        return o_all.at[window(relative[r], width), window(s, part)]
 
     def send_block(r, s):
         return remote(
@@ -420,16 +446,10 @@
     for r in (2, 3, 1):
         send_block(r, step).start()
     keep_block(step).start()
-
     slots(3)
 
-    @pl.when(step == count - 1)
+    @pl.when(step == last)
     def _():
-        wt[3 * width :] = pt[0 : 3 * RANK]
-        for j in range(3):
-            part_j = slice(j * width, (j + 1) * width)
-            delta = nn(up_t[part_j], pt[0 : 3 * RANK])
-            wt[part_j] = (w_ref[j].astype(F32) + LOWRANK * delta).astype(BF16)
         to_head(1, later).wait_recv()
         pass_on(later).wait_recv()
         tile_a[...] = natural(1)
@@ -443,7 +463,121 @@
                 base = (w * split + k) * rows
                 unpack[base : base + rows] = jnp.concatenate(blocks, axis=1)
         bt[...] = unpack[...].T.astype(BF16)
-        finish(2, (3, 4))
+        ta = tile_a[...].T.astype(BF16)
+        p3t, p4t, p8t, p9t = (ta[m * RANK : (m + 1) * RANK] for m in range(4))
+        p3 = tile_a[:, 0:RANK].astype(BF16)
+
+        def inner_at(q, r):
+            start = pl.multiple_of(relative[r] * 2 * RANK, 2 * RANK) + q * RANK
+            return pl.ds(start, RANK)
+
+        for w in range(3):
+            keep_w(w).wait()
+        own_rows().wait()
+        for w in range(3):
+            sibling_own(w).wait_recv()
+        sibling_far(0).wait_recv()
+
+        def project(first, pairs):
+            tokens_here = slice(first * part, (first + pairs) * part)
+            for s in range(first, first + pairs):
+                keep_block(s).wait()
+                for r in range(1, nh):
+                    arrive_block(r, s).wait_recv()
+            ocat[tokens_here] = o_all[:, tokens_here].T
+            z = nt(ocat[tokens_here], p3t).astype(BF16)
+            v = (
+                x[first : first + pairs].reshape(pairs * part, model).astype(F32)
+                + nn(ocat[tokens_here], wo[...])
+                + nn(z, p8t) * LOWRANK
+                + shifts[0:1]
+            )
+            n, inv = centred(v)
+            n1[tokens_here] = n
+            i1[tokens_here] = inv
+            h1[tokens_here] = n * gains[0:1] + shifts[1:2]
+            h1b[tokens_here] = h1[tokens_here].astype(BF16)
+            return z
+
+        z_o = jnp.concatenate([project(0, count - 1), project(count - 1, 1)], axis=0)
+        relay(4)
+        z_up = nt(h1b[...], p4t).astype(BF16)
+        chunk = 256
+        z_d = jnp.zeros((tokens, RANK), F32)
+        for r in range(nh):
+            if r == 2:
+                finish(2, (3, 4))
+            if r == 3:
+                sibling_far(1).wait_recv()
+
+            def up(c, carry, r=r):
+                cols = window(c, chunk)
+                q1 = bt[inner_at(1, r), cols] * jnp.asarray(LOWRANK, BF16)
+                bias_at = pl.ds(
+                    pl.multiple_of(relative[r] * model + c * chunk, chunk), chunk
+                )
+                a = nn(h1b[...], wu[r, :, cols]) + nn(z_up, q1) + up_bias[0:1, bias_at]
+                cdf, density = cdf_and_density(a)
+                f[r, :, cols] = (a * cdf).astype(BF16)
+                slope[r, :, cols] = (cdf + a * density).astype(BF16)
+                return carry
+
+            lax.fori_loop(0, model // chunk, up, 0)
+            z_d = z_d + nt(f[r], bt[inner_at(0, r), :])
+        z_d = z_d.astype(BF16)
+        for r in range(nh):
+            if r == 3:
+                sibling_far(2).wait_recv()
+            term = nn(f[r], wd[r])
+            if r == 0:
+                acc[...] = term + nn(z_d, p9t) * LOWRANK
+            else:
+                acc[...] += term
+        n2, i2 = centred(h1[...] + acc[...] + shifts[2:3])
+        result[...] = (n2 * gains[1:2] + shifts[3:4]).astype(BF16).reshape(result.shape)
+        give_result = pltpu.make_async_copy(result, result_out, store.at[0])
+        give_result.start()
+        e = gout[...].reshape(tokens, model).astype(F32) * gains[1:2]
+        r2[...] = norm_back(e, n2, i2)
+        gf[...] = r2[...].astype(BF16)
+        gzd = (nt(gf[...], p9t) * LOWRANK).astype(BF16)
+        g9 = tn(z_d, gf[...]) * LOWRANK
+        gzu = jnp.zeros((tokens, RANK), F32)
+        for r in range(nh):
+            gbt[inner_at(0, r), :] = tn(gzd, f[r])
+
+            def down(c, carry, r=r):
+                cols = window(c, chunk)
+                df = nt(gf[...], wd[r, cols, :]) + nn(gzd, bt[inner_at(0, r), cols])
+                slope[r, :, cols] = (df * slope[r, :, cols].astype(F32)).astype(BF16)
+                return carry
+
+            lax.fori_loop(0, model // chunk, down, 0)
+            ga = slope[r]
+            gzu = gzu + nt(ga, bt[inner_at(1, r), :])
+            gbt[inner_at(1, r), :] = tn(z_up, ga) * LOWRANK
+            term = nt(ga, wu[r])
+            if r == 0:
+                acc[...] = r2[...] + term
+            else:
+                acc[...] += term
+        gzu = (gzu * LOWRANK).astype(BF16)
+        g4 = tn(gzu, h1b[...])
+        e = (acc[...] + nn(gzu, p4t)) * gains[0:1]
+        gat[...] = norm_back(e, n1[...], i1[...]).astype(BF16)
+        give_gat = pltpu.make_async_copy(gat, gat_out, store.at[1])
+        give_gat.start()
+        gzo = (nt(gat[...], p8t) * LOWRANK).astype(BF16)
+        go[...] = (nt(wo[...], gat[...]) + nt(p3, gzo)).astype(BF16)
+        give_go = pltpu.make_async_copy(go, go_out, store.at[2])
+        give_go.start()
+        g8 = tn(z_o, gat[...]) * LOWRANK
+        g3 = tn(gzo, ocat[...])
+        zeros = jnp.zeros((4 * RANK, model), F32)
+        grads[0] = jnp.concatenate([g3, g4, g8, g9, zeros], axis=0).T
+        grads[1] = gbt[...].T
+        give_grads = pltpu.make_async_copy(grads, grads_out, store.at[3])
+        give_grads.start()
         for c in range(len(chunks)):
             over_x(c).wait_send()
             for axis in (1, 2):
@@ -456,49 +590,56 @@
                 to_head(b, slot).wait_send()
             pass_on(slot).wait_send()
         for s in range(count):
-            keep_block(s).wait()
             for r in range(1, nh):
                 send_block(r, s).wait_send()
-                arrive_block(r, s).wait_recv()
         for w in range(3):
-            sibling_own(w).wait()
-            sibling_far(w).wait()
-
-
-def attend(nd, nh, hidden, lengths, adapters_m, adapters_i, weight, bias, wo, wu, wd):
+            sibling_own(w).wait_send()
+            sibling_far(w).wait_send()
+        for give in (give_result, give_gat, give_go, give_grads):
+            give.wait()
+
+
+def forward(
+    nd, nh, hidden, lengths, adapters_m, adapters_i, weight, bias, wo, wu, wd, gout, shifts,
+    gains, up_bias,
+):
     count, keys, model = hidden.shape
     width = weight.shape[1]
     heads = width // DH
     tall = 3 * width + 3 * RANK
     part = keys // nh
+    tokens = count * part
     rows = adapters_m.shape[2]
     padded = -(-rows // 8) * 8
     shape = jax.ShapeDtypeStruct
     dma = pltpu.SemaphoreType.DMA
     return pl.pallas_call(
-        functools.partial(attend_kernel, nd, nh),
+        functools.partial(forward_kernel, nd, nh),
         grid=(count,),
         in_specs=[
             pl.BlockSpec(memory_space=pltpu.SMEM),
-            vmem(), vmem(), anywhere(), vmem(), vmem(), anywhere(), anywhere(), anywhere(),
+            vmem(), vmem(),
+            pl.BlockSpec((1, keys, model), lambda s: (s, 0, 0)),
+            anywhere(), vmem(), vmem(), anywhere(), anywhere(), anywhere(),
+            vmem(), vmem(), vmem(), vmem(),
         ],
         out_specs=[
             pl.BlockSpec((1, tall, keys), lambda s: (s, 0, 0)),
             pl.BlockSpec((1, heads, keys, keys), lambda s: (s, 0, 0, 0)),
             pl.BlockSpec((1, heads, keys), lambda s: (s, 0, 0)),
+            vmem(), vmem(),
             anywhere(), anywhere(), anywhere(), anywhere(),
-            vmem(), vmem(), vmem(), vmem(),
         ],
         out_shape=[
             shape((count, tall, keys), BF16),
             shape((count, heads, keys, keys), BF16),
             shape((count, heads, keys), F32),
-            shape((nh * width, count * part), BF16),
-            *[shape((nh - 1, *w.shape), BF16) for w in (wo, wu, wd)],
             shape((tall, model), BF16),
-            shape((model, LANES), F32),
-            shape((LANES, model), BF16),
             shape((LANES, width), BF16),
+            shape((count, part, model), BF16),
+            shape((tokens, model), BF16),
+            shape((model, tokens), BF16),
+            shape((2, model, LANES), F32),
         ],
         scratch_shapes=[
             pltpu.VMEM((3, padded, LANES), F32),
@@ -507,191 +648,14 @@
             pltpu.VMEM((count, width, keys), BF16),
             pltpu.VMEM((model, 8), F32),
             pltpu.VMEM((model, LANES), F32),
-            pltpu.VMEM((count, keys, model), BF16),
-            pltpu.VMEM((count, 3 * width, keys), F32),
-            pltpu.VMEM((3 * width, 3 * RANK), BF16),
+            pltpu.VMEM((model, LANES), F32),
             pltpu.VMEM((LANES, model), BF16),
-            dma((count,)),
-            dma((2, nd)), dma((2, nd)), dma((2, 4)), dma((2, 4)),
-            dma((nh, count)), dma((nh, count)), dma((count,)),
-            dma((5, 5)), dma((5, 5)), dma((2, 3)), dma((2, 3)),
-        ],
-        compiler_params=pltpu.CompilerParams(
-            collective_id=1, has_side_effects=True, vmem_limit_bytes=VMEM_LIMIT
-        ),
-        name="attend",
-    )(lengths, adapters_m, adapters_i, hidden, weight, bias, wo, wu, wd)
-
-
-def tail_density(a):
-    e = jnp.exp(-0.5 * a * a)
-    t = 1.0 / (1.0 + (0.3275911 * 0.7071067811865476) * jnp.abs(a))
-    poly = 1.061405429 * t - 1.453152027
-    poly = poly * t + 1.421413741
-    poly = poly * t - 0.284496736
-    poly = poly * t + 0.254829592
-    q = (0.5 * poly * t) * e
-    return jnp.where(a >= 0, 1.0 - q, q), e * 0.3989422804014327
-
-
-def centred(v):
-    c = v - jnp.mean(v, axis=-1, keepdims=True)
-    inverse = lax.rsqrt(jnp.mean(c * c, axis=-1, keepdims=True) + EPS_NORM)
-    return c * inverse, inverse
-
-
-def norm_back(e, n, inverse):
-    return inverse * (
-        e - jnp.mean(e, axis=-1, keepdims=True) - n * jnp.mean(e * n, axis=-1, keepdims=True)
-    )
-
-
-def token_kernel(
-    nh, o_all, x_hbm, gout, wo_own, wo_rest, wu_own, wu_rest, wd_own, wd_rest,
-    tile_a, bt, shifts, gains, up_bias,
-    result, first, go, grads,
-    x, wo, ocat, wu, wd, f, slope, h1, n1, i1, h1b, r2, gf, acc, gat, gbt, sem_x, sem_w,
-):
-    h = lax.axis_index("head")
-    pairs, part, model = x.shape
-    tokens = pairs * part
-    width = wo_own.shape[0]
-    relative = [jnp.bitwise_xor(h, r) for r in range(nh)]
-    own = pltpu.make_async_copy(
-        x_hbm.at[:, pl.ds(pl.multiple_of(h * part, part), part), :], x, sem_x
-    )
-    own.start()
-    fetch = []
-    for r in range(nh):
-        a = wu_own if r == 0 else wu_rest.at[r - 1]
-        b = wd_own if r == 0 else wd_rest.at[r - 1]
-        fetch.append(
-            (
-                pltpu.make_async_copy(a, wu.at[r], sem_w.at[0, r]),
-                pltpu.make_async_copy(b, wd.at[r], sem_w.at[1, r]),
-            )
-        )
-    for r in range(nh):
-        fetch[r][0].start()
-    for r in range(nh):
-        fetch[r][1].start()
-    ocat[...] = o_all[...].T
-    for r in range(nh):
-        rows = pl.ds(pl.multiple_of(relative[r] * width, width), width)
-        wo[rows] = wo_own[...] if r == 0 else wo_rest[r - 1]
-    at = tile_a[...].T.astype(BF16)
-    p3t, p4t, p8t, p9t = (at[m * RANK : (m + 1) * RANK] for m in range(4))
-    p3 = tile_a[:, 0:RANK].astype(BF16)
-
-    def inner(q, r):
-        return bt[pl.ds(pl.multiple_of(relative[r] * 2 * RANK, 2 * RANK) + q * RANK, RANK), :]
-
-    z_o = nt(ocat[...], p3t).astype(BF16)
-    acc[...] = nn(ocat[...], wo[...]) + nn(z_o, p8t) * LOWRANK
-    own.wait()
-    v = x[...].reshape(tokens, model).astype(F32) + acc[...] + shifts[0:1]
-    n, inv = centred(v)
-    n1[...] = n
-    i1[...] = inv
-    h1[...] = n * gains[0:1] + shifts[1:2]
-    h1b[...] = h1[...].astype(BF16)
-    z_up = nt(h1b[...], p4t).astype(BF16)
-    chunk = 256
-    z_d = jnp.zeros((tokens, RANK), F32)
-    for r in range(nh):
-        fetch[r][0].wait()
-
-        def up(c, carry, r=r):
-            cols = pl.ds(pl.multiple_of(c * chunk, chunk), chunk)
-            q1 = bt[
-                pl.ds(pl.multiple_of(relative[r] * 2 * RANK, 2 * RANK) + RANK, RANK), cols
-            ]
-            a = (
-                nn(h1b[...], wu[r, :, cols])
-                + nn(z_up, q1) * LOWRANK
-                + up_bias[pl.ds(relative[r], 1), cols]
-            )
-            cdf, density = tail_density(a)
-            f[r, :, cols] = (a * cdf).astype(BF16)
-            slope[r, :, cols] = (cdf + a * density).astype(BF16)
-            return carry
-
-        lax.fori_loop(0, model // chunk, up, 0)
-        z_d = z_d + nt(f[r], inner(0, r))
-    z_d = z_d.astype(BF16)
-    for r in range(nh):
-        fetch[r][1].wait()
-        term = nn(f[r], wd[r])
-        if r == 0:
-            acc[...] = term + nn(z_d, p9t) * LOWRANK
-        else:
-            acc[...] += term
-    n2, i2 = centred(h1[...] + acc[...] + shifts[2:3])
-    result[...] = (n2 * gains[1:2] + shifts[3:4]).astype(BF16).reshape(result.shape)
-    e = gout[...].reshape(tokens, model).astype(F32) * gains[1:2]
-    r2[...] = norm_back(e, n2, i2)
-    gf[...] = r2[...].astype(BF16)
-    gzd = (nt(gf[...], p9t) * LOWRANK).astype(BF16)
-    g9 = tn(z_d, gf[...]) * LOWRANK
-    gzu = jnp.zeros((tokens, RANK), F32)
-    for r in range(nh):
-        gbt[pl.ds(pl.multiple_of(relative[r] * 2 * RANK, 2 * RANK), RANK), :] = tn(gzd, f[r])
-
-        def down(c, carry, r=r):
-            cols = pl.ds(pl.multiple_of(c * chunk, chunk), chunk)
-            q0 = bt[pl.ds(pl.multiple_of(relative[r] * 2 * RANK, 2 * RANK), RANK), cols]
-            df = nt(gf[...], wd[r, cols, :]) + nn(gzd, q0)
-            slope[r, :, cols] = (df * slope[r, :, cols].astype(F32)).astype(BF16)
-            return carry
-
-        lax.fori_loop(0, model // chunk, down, 0)
-        ga = slope[r]
-        gzu = gzu + nt(ga, inner(1, r))
-        gbt[pl.ds(pl.multiple_of(relative[r] * 2 * RANK, 2 * RANK) + RANK, RANK), :] = (
-            tn(z_up, ga) * LOWRANK
-        )
-        term = nt(ga, wu[r])
-        if r == 0:
-            acc[...] = r2[...] + term
-        else:
-            acc[...] += term
-    gzu = (gzu * LOWRANK).astype(BF16)
-    g4 = tn(gzu, h1b[...])
-    e = (acc[...] + nn(gzu, p4t)) * gains[0:1]
-    r1 = norm_back(e, n1[...], i1[...])
-    first[...] = r1.reshape(first.shape)
-    gat[...] = r1.astype(BF16)
-    gzo = (nt(gat[...], p8t) * LOWRANK).astype(BF16)
-    g8 = tn(z_o, gat[...]) * LOWRANK
-    g3 = tn(gzo, ocat[...])
-    go[...] = (nt(wo[...], gat[...]) + nt(p3, gzo)).astype(BF16)
-    zeros = jnp.zeros((4 * RANK, model), F32)
-    grads[0] = jnp.concatenate([g3, g4, g8, g9, zeros], axis=0).T
-    grads[1] = gbt[...].T
-
-
-def token_side(o_all, hidden, gout, wo, wu, wd, tile_a, bt, shifts, gains, up_bias):
-    pairs, part, model = gout.shape
-    tokens = pairs * part
-    width = wo[0].shape[0]
-    nh = model // width
-    shape = jax.ShapeDtypeStruct
-    return pl.pallas_call(
-        functools.partial(token_kernel, nh),
-        out_shape=[
-            shape((pairs, part, model), BF16),
-            shape((pairs, part, model), F32),
-            shape((model, tokens), BF16),
-            shape((2, model, LANES), F32),
-        ],
-        in_specs=[vmem(), anywhere(), vmem(), vmem(), vmem()] + [anywhere()] * 4 + [vmem()] * 5,
-        out_specs=[vmem()] * 4,
-        scratch_shapes=[
-            pltpu.VMEM((pairs, part, model), BF16),
+            pltpu.VMEM((model, tokens), BF16),
             pltpu.VMEM((model, model), BF16),
-            pltpu.VMEM((tokens, model), BF16),
             pltpu.VMEM((nh, model, model), BF16),
             pltpu.VMEM((nh, model, model), BF16),
+            pltpu.VMEM((count, part, model), BF16),
+            pltpu.VMEM((tokens, model), BF16),
             pltpu.VMEM((nh, tokens, model), BF16),
             pltpu.VMEM((nh, tokens, model), BF16),
             pltpu.VMEM((tokens, model), F32),
@@ -703,12 +667,22 @@
             pltpu.VMEM((tokens, model), F32),
             pltpu.VMEM((tokens, model), BF16),
             pltpu.VMEM((LANES, model), F32),
-            pltpu.SemaphoreType.DMA,
-            pltpu.SemaphoreType.DMA((2, nh)),
+            pltpu.VMEM((count, part, model), BF16),
+            pltpu.VMEM((model, tokens), BF16),
+            pltpu.VMEM((2, model, LANES), F32),
+            dma((2, nd)), dma((2, nd)), dma((2, 4)), dma((2, 4)),
+            dma((nh, count)), dma((nh, count)), dma((count,)),
+            dma((5, 5)), dma((5, 5)), dma((2, 3)), dma((2, 3)),
+            dma((4,)), dma((4,)),
         ],
-        compiler_params=pltpu.CompilerParams(vmem_limit_bytes=VMEM_LIMIT),
-        name="token_side",
-    )(o_all, hidden, gout, *wo, *wu, *wd, tile_a, bt, shifts, gains, up_bias)
+        compiler_params=pltpu.CompilerParams(
+            collective_id=1, has_side_effects=True, vmem_limit_bytes=VMEM_LIMIT
+        ),
+        name="forward",
+    )(
+        lengths, adapters_m, adapters_i, hidden, hidden, weight, bias, wo, wu, wd, gout, shifts,
+        gains, up_bias,
+    )
 
 
 def attend_back_kernel(
@@ -771,7 +745,7 @@
         to_near(0, s).wait_recv()
         to_far(s).wait_recv()
         grad_in[s] = (
-            first[s]
+            first[s].astype(F32)
             + whole_buf[s, h].astype(F32)
             + near[s, 0].astype(F32)
             + last[s].astype(F32)
@@ -811,6 +785,12 @@
         gproj[part_h] = nn(kt, gst).astype(BF16)
         gproj[rows_k] = nt(qt, gst).astype(BF16)
         gproj[rows_v] = nt(gs, et).astype(BF16)
+        if head == 0:
+
+            @pl.when(step == 2)
+            def _():
+                two.over_head(0)
+
         if head == 1:
 
             @pl.when(step >= 1)
@@ -834,10 +814,6 @@
         two.over_dp()
 
     @pl.when(step == 2)
-    def _():
-        two.over_head(0)
-
-    @pl.when(step == 3)
     def _():
         two.over_head(1)
 
@@ -879,8 +855,9 @@
                 blocks[2, m * RANK : (m + 1) * RANK, m * RANK : (m + 1) * RANK] = roots_r[
                     roots_m.shape[0] + q
                 ]
+        one.over_dp()
         two.finish(gradients.at[1:3])
-        one.over_dp()
+        one.over_head(0)
         mix(1)
         mix(2)
         for q in range(2):
@@ -892,9 +869,8 @@
                     roots_i[q, :, k * model : (k + 1) * model].astype(BF16),
                 )
             preconditioned(roots_m.shape[0] + q, u, step_i, q)
-        one.over_head(0)
+        one.over_head(1)
         steps_model(1)
-        one.over_head(1)
         for s in range(count):
             complete(s)
         one.finish(gradients.at[0:1])
@@ -1092,18 +1068,14 @@
     model = hidden_input.shape[2]
     turned_m = jnp.swapaxes(adapters_model, 1, 2)
     turned_i = jnp.swapaxes(adapters_inner, 1, 2)
-    proj, p, inverse, o_all, wo_rest, wu_rest, wd_rest, wt, tile_a, bt, down_t = attend(
+    proj, p, inverse, wt, down_t, result, gat, go, early = forward(
         nd, nh, hidden_input, pair_lengths, turned_m, turned_i,
         jnp.swapaxes(query_key_value_weight, 1, 2), qkv_bias,
         output_projection_weight, up_projection_weight, down_projection_weight,
-    )
-    result, first, go, early = token_side(
-        o_all, hidden_input, grad_out,
-        (output_projection_weight, wo_rest), (up_projection_weight, wu_rest),
-        (down_projection_weight, wd_rest), tile_a, bt, shifts, gains, up_bias.reshape(nh, model),
+        grad_out, shifts, gains, up_bias.reshape(1, -1),
     )
     grad_in, gradients, step_m, step_i, squares = attend_back(
-        nd, nh, hidden_input, proj, p, inverse, go, first, early, wt, down_t,
+        nd, nh, hidden_input, proj, p, inverse, go, gat.reshape(grad_out.shape), early, wt, down_t,
         roots_model, roots_inner, roots_rank,
     )
     grad_in, grad_m, grad_i, adapt_m, adapt_i, new_m, new_i, new_r = finish(

time: 166 us -> 150 us (0.904)
  Pallas kernels: 164 us -> 148 us
    pallas_call x2 -> x1, Pallas kernels: 94.6 us -> 83 us  [forward(): pl.pallas_call(functools.partial(forward_kernel, nd, nh), grid=(count,),...]
    pallas_call x1, Pallas kernels: 63.7 us -> 59.3 us  [attend_back(): pl.pallas_call(functools.partial(attend_back_kernel, nd, nh), grid=(count...]
where the time goes in v1:
time: 150 us; the launch traced here: 149 us
  Pallas kernels  148 us (99%)
    pallas_call x1, Pallas kernels, forward(): pl.pallas_call(functools.partial(forward_kernel, nd, nh), grid=(count,),...  83 us
    pallas_call x1, Pallas kernels, attend_back(): pl.pallas_call(functools.partial(attend_back_kernel, nd, nh), grid=(count...  59.3 us
    pallas_call x1, Pallas kernels, finish(): pl.pallas_call(functools.partial(finish_kernel, nh, nd * nh), in_specs=[v...  5.46 us

profile of v1, /device:TPU:0, one launch (start us, length us, event | category | flops | bytes accessed | tf_op | source)
XLA Modules:
  0.0 149.4 jit_solution(6409081286109017585)
XLA Ops:
  0.6 83.0 %forward.1 = (bf16[5,624,512]{2,1,0:T(8,128)(2,1)}, bf16[5,3,512,512]{3,2,1,0:T(8,128)(2,1)}, f32[5,3,512]{2,1,0:T(4,128)}, bf16[624,768]{1,0:T(8,128)(2,1)}, bf...) custom-call(s32[5]{0:T(128)} %lengths.1, ...), custom_call_target="tpu_custom_call" | custom-call | tf_op jit(solution)/shard_map/forward/pallas_call | solution.py:616
  83.6 59.3 %attend_back.1 = (bf16[5,128,768]{2,1,0:T(8,128)(2,1)}, f32[3,768,128]{2,1,0:T(8,128)}, f32[10,16,24]{2,1,0:T(8,128)}, f32[2,16,96]{2,1,0:T(8,128)}, f32[16,128]{1,0:T(8,128)}) custom-call(bf16[5,512,768]{2,1,0:T(8,128)(2,1)} %x_ref.3, bf16[5,624,512]{2,1,0:T(8,128)(2,1)} %get-tuple-element.32.proj_ref, bf16[5,3,512,512]{3,2,1,0:T(8,128)(2,1)} %get-tuple-element.33.p_ref, ...), custom_call_target="tpu_custom_call" | custom-call | tf_op jit(solution)/shard_map/attend_back/pallas_call | solution.py:926
  143.0 0.0 copy-start
  143.0 5.5 %finish.1 = (bf16[5,128,768]{2,1,0:T(8,128)(2,1)}, f32[10,16,24]{2,1,0:T(8,128)}, f32[2,16,96]{2,1,0:T(8,128)}, f32[10,16,24]{2,1,0:T(8,128)}, f32[2,16,96]{2,1,...) custom-call(bf16[5,128,768]{2,1,0:T(8,128)(2,1)} %get-tuple-element.40.grad_in, ...), custom_call_target="tpu_custom_call" | custom-call | tf_op jit(solution)/shard_map/finish/pallas_call | solution.py:1025
  148.4 0.0 copy-done
  148.5 0.9 copy.29
Async XLA Ops:
  143.0 5.5 %copy-start = (bf16[5,128,768]{2,1,0:T(8,128)(2,1)S(1)}, bf16[5,128,768]{2,1,0:T(8,128)(2,1)}, u32[]{:S(2)}) copy-start(bf16[5,128,768]{2,1,0:T(8,128)(2,1)} %get-tuple-element.62) | copy-start | bytes 2949124

commit v2 on v1

--- a/solution.py
+++ b/solution.py
@@ -17,6 +17,7 @@
 EPS_NORM = 1e-5
 MESH = pl.DeviceIdType.MESH
 VMEM_LIMIT = 60 << 20
+AHEAD = 3
 F32 = jnp.float32
 BF16 = jnp.bfloat16
 HIGH = lax.Precision.HIGHEST
@@ -100,10 +101,10 @@
             [
                 pltpu.VMEM((nd, tiles, rows, LANES), BF16),
                 pltpu.VMEM((nd, tiles, rows, LANES), BF16),
-                pltpu.VMEM((4, tiles, rows, LANES), BF16),
+                pltpu.VMEM((nh, tiles, rows, LANES), BF16),
                 pltpu.VMEM((nd, tiles, rows, LANES), BF16),
             ],
-            [dma((nd,)), dma((nd,)), dma((2,)), dma((2,)), dma((nd,)), dma((nd,))],
+            [dma((nd,)), dma((nd,)), dma((nh,)), dma((nh,)), dma((nd,)), dma((nd,))],
         )
 
     def to_owner(self, k):
@@ -113,10 +114,11 @@
             (peer, self.h),
         )
 
-    def across(self, i):
-        return remote(
-            self.near.at[2 * i], self.near.at[2 * i + 1], self.sems[2].at[i],
-            self.sems[3].at[i], (self.d, jnp.bitwise_xor(self.h, i + 1)),
+    def across(self, r):
+        here = self.near.at[self.h]
+        return remote(
+            here, here, self.sems[2].at[r], self.sems[3].at[r],
+            (self.d, jnp.bitwise_xor(self.h, r)),
         )
 
     def to_all(self, k):
@@ -138,19 +140,19 @@
         for k in range(1, self.nd):
             self.to_owner(k).wait_recv()
             total = total + self.part[k].astype(F32)
-        self.near[0] = total.astype(BF16)
-        self.across(0).start()
-
-    def over_head(self, i):
-        self.across(i).wait_recv()
-        total = self.near[2 * i].astype(F32) + self.near[2 * i + 1].astype(F32)
-        if i == 0:
-            self.near[2] = total.astype(BF16)
-            self.across(1).start()
-        else:
-            self.full[self.d] = total.astype(BF16)
-            for k in range(1, self.nd):
-                self.to_all(k).start()
+        self.near[self.h] = total.astype(BF16)
+        for r in range(self.nh - 1, 0, -1):
+            self.across(r).start()
+
+    def over_head(self):
+        for r in range(1, self.nh):
+            self.across(r).wait_recv()
+        total = self.near[0].astype(F32)
+        for source in range(1, self.nh):
+            total = total + self.near[source].astype(F32)
+        self.full[self.d] = total.astype(BF16)
+        for k in range(1, self.nd):
+            self.to_all(k).start()
 
     def finish(self, target):
         size = target.shape[1] // self.nd
@@ -161,8 +163,8 @@
         for k in range(1, self.nd):
             self.to_owner(k).wait_send()
             self.to_all(k).wait_send()
-        for i in range(2):
-            self.across(i).wait_send()
+        for r in range(1, self.nh):
+            self.across(r).wait_send()
 
 
 def cdf_and_density(a):
@@ -185,11 +187,11 @@
 def forward_kernel(
     nd, nh, lengths, am, ai, x_ref, x_hbm, w_ref, bias_ref, wo_own, wu_own, wd_own,
     gout, shifts, gains, up_bias,
-    proj_ref, p_ref, inv_ref, wt, down_t, result_out, gat_out, go_out, grads_out,
-    packed, first_tile, other_tiles, obuf, bias_col, unpack, tile_a, bt,
+    proj_ref, p_ref, inv_ref, wt, down_t, result_out, gat_out, go_out, grads_out, got_out,
+    packed, packed_more, first_tile, other_tiles, obuf, bias_col, unpack, tile_a, bt,
     o_all, wo, wu, wd, x, ocat, f, slope, h1, n1, i1, h1b, r2, gf, acc, gat, gbt, result, go, grads,
     send_d, recv_d, send_h, recv_h, send_o, recv_o, keep_o, send_w, recv_w, send_s, recv_s,
-    load, store,
+    load, store, send_g, recv_g, keep_g,
 ):
     step = pl.program_id(0)
     last = pl.num_programs(0) - 1
@@ -285,7 +287,7 @@
         sibling_far(w).start()
 
     stores = (first_tile, other_tiles)
-    sources = (packed.at[pl.ds(0, 1)], packed.at[pl.ds(1, 2)])
+    sources = (packed, packed_more)
     critical, later = 0, 1
 
     def to_dp(k, slot):
@@ -304,8 +306,9 @@
 
     def entry(t, owner):
         if t == 0:
-            return first_tile[owner % nh, owner // nh, 0, 0:rows]
-        return other_tiles[owner % nh, owner // nh, t - 1, 0:rows]
+            return first_tile[owner % nh, owner // nh].astype(F32)[0:rows]
+        both = other_tiles[owner % nh, owner // nh].astype(F32)
+        return both[(t - 1) * rows : t * rows]
 
     def natural(t):
         return jnp.concatenate([entry(t, i) for i in range(owners)], axis=0)
@@ -326,24 +329,28 @@
     @pl.when(step == 0)
     def _():
         greet_signal(nd, nh)
-        packed[...] = jnp.zeros_like(packed)
         groups = [
             [am[j] for j in EARLY_SLOTS],
             [am[j] for j in LATE_SLOTS],
             [ai[q][:, k * rows : (k + 1) * rows] for k in range(split) for q in range(2)],
         ]
-        for t, group in enumerate(groups):
+        turned = []
+        for group in groups:
             short = LANES - len(group) * RANK
             if short:
                 group = group + [jnp.zeros((short, rows), F32)]
-            packed[t, 0:rows] = jnp.concatenate(group, axis=0).T.astype(BF16).astype(F32)
-        first_tile[h, d] = packed[0:1]
-        other_tiles[h, d] = packed[1:3]
+            turned.append(jnp.concatenate(group, axis=0).T)
+        for target, parts in ((packed, turned[0:1]), (packed_more, turned[1:3])):
+            short = target.shape[0] - len(parts) * rows
+            if short:
+                parts = parts + [jnp.zeros((short, LANES), F32)]
+            target[...] = jnp.concatenate(parts, axis=0).astype(BF16)
+        first_tile[h, d] = packed[...]
+        other_tiles[h, d] = packed_more[...]
         greet_wait(nd, nh)
         for k in range(1, nd):
             to_dp(k, critical).start()
         over_x(0).start()
-        over_x(1).start()
         bias_col[...] = jnp.concatenate(
             [bias_ref[...], jnp.zeros((5, model), F32)], axis=0
         ).T
@@ -351,16 +358,12 @@
             to_dp(k, critical).wait_recv()
         to_head(2, critical).start()
         to_head(1, critical).start()
-        for c in range(2, len(chunks)):
-            over_x(c).start()
-        for w in range(3):
-            sibling_own(w).start()
-            keep_w(w).start()
-        own_rows().start()
         to_head(2, critical).wait_recv()
         pass_on(critical).start()
         to_head(1, critical).wait_recv()
         pass_on(critical).wait_recv()
+        over_x(1).start()
+        over_x(2).start()
         pn = natural(0)
         pt = pn.T.astype(BF16)
         tile_a[...] = pn
@@ -375,6 +378,10 @@
             )
         for k in range(1, nd):
             to_dp(k, later).start()
+        for w in range(3):
+            sibling_own(w).start()
+            keep_w(w).start()
+        own_rows().start()
 
     proj = nt(wt[...], x_ref[0])
     mine = window(h, width)
@@ -387,15 +394,11 @@
 
     bind = functools.partial
     plan = {
-        (0, 0): [bind(forward, 0)],
-        (0, 1): [bind(forward, 1)],
-        (1, 1): [bind(forward, 2), bind(relay, 0)],
-        (1, 3): [later_to_head, bind(relay, 1)],
-        (2, 1): [bind(finish, 0, (0,))],
-        (2, 3): [bind(forward, 3), bind(relay, 2)],
-        (3, 1): [later_pass_on],
-        (3, 3): [bind(finish, 1, (1, 2)), bind(forward, 4)],
-        (4, 1): [bind(relay, 3)],
+        (0, 3): [bind(forward, 0), bind(forward, 1)],
+        (1, 3): [later_to_head, bind(relay, 0), bind(forward, 2)],
+        (2, 3): [bind(relay, 1), bind(finish, 0, (0,))],
+        (3, 3): [later_pass_on, bind(relay, 2)],
+        (4, 3): [bind(finish, 1, (1, 2)), over_x(3).start, over_x(4).start],
     }
 
     def slots(place):
@@ -409,7 +412,6 @@
 
     results = []
     for head in range(width // DH):
-        slots(head)
         rows_q = slice(head * DH, (head + 1) * DH)
         qt = proj_ref[0, rows_q] * jnp.asarray(DH ** (-0.5), BF16)
         kt = proj_ref[0, width + head * DH : width + (head + 1) * DH]
@@ -447,6 +449,7 @@
         send_block(r, step).start()
     keep_block(step).start()
     slots(3)
+
 
     @pl.when(step == last)
     def _():
@@ -499,15 +502,19 @@
             h1b[tokens_here] = h1[tokens_here].astype(BF16)
             return z
 
-        z_o = jnp.concatenate([project(0, count - 1), project(count - 1, 1)], axis=0)
-        relay(4)
+        z_o = project(0, count - 1)
+        z_o = jnp.concatenate([z_o, project(count - 1, 1)], axis=0)
+        forward(3)
         z_up = nt(h1b[...], p4t).astype(BF16)
         chunk = 256
         z_d = jnp.zeros((tokens, RANK), F32)
         for r in range(nh):
+            if r == 1:
+                forward(4)
             if r == 2:
-                finish(2, (3, 4))
+                relay(3)
             if r == 3:
+                relay(4)
                 sibling_far(1).wait_recv()
 
             def up(c, carry, r=r):
@@ -522,8 +529,9 @@
                 slope[r, :, cols] = (cdf + a * density).astype(BF16)
                 return carry
 
-            lax.fori_loop(0, model // chunk, up, 0)
+            lax.fori_loop(0, model // chunk, up, 0, unroll=True)
             z_d = z_d + nt(f[r], bt[inner_at(0, r), :])
+        finish(2, (3, 4))
         z_d = z_d.astype(BF16)
         for r in range(nh):
             if r == 3:
@@ -542,37 +550,64 @@
         gf[...] = r2[...].astype(BF16)
         gzd = (nt(gf[...], p9t) * LOWRANK).astype(BF16)
         g9 = tn(z_d, gf[...]) * LOWRANK
-        gzu = jnp.zeros((tokens, RANK), F32)
         for r in range(nh):
             gbt[inner_at(0, r), :] = tn(gzd, f[r])
 
-            def down(c, carry, r=r):
-                cols = window(c, chunk)
-                df = nt(gf[...], wd[r, cols, :]) + nn(gzd, bt[inner_at(0, r), cols])
-                slope[r, :, cols] = (df * slope[r, :, cols].astype(F32)).astype(BF16)
-                return carry
-
-            lax.fori_loop(0, model // chunk, down, 0)
-            ga = slope[r]
-            gzu = gzu + nt(ga, bt[inner_at(1, r), :])
-            gbt[inner_at(1, r), :] = tn(z_up, ga) * LOWRANK
-            term = nt(ga, wu[r])
-            if r == 0:
-                acc[...] = r2[...] + term
-            else:
-                acc[...] += term
-        gzu = (gzu * LOWRANK).astype(BF16)
-        g4 = tn(gzu, h1b[...])
-        e = (acc[...] + nn(gzu, p4t)) * gains[0:1]
-        gat[...] = norm_back(e, n1[...], i1[...]).astype(BF16)
+        def send_go(r, s):
+            return remote(
+                go.at[window(relative[r], width), window(s, part)],
+                got_out.at[s, :, window(h, part)],
+                send_g.at[r, s], recv_g.at[r, s], at(0, r),
+            )
+
+        def keep_go(s):
+            return pltpu.make_async_copy(
+                go.at[window(h, width), window(s, part)],
+                got_out.at[s, :, window(h, part)],
+                keep_g.at[s],
+            )
+
+        g3, g4, g8 = (jnp.zeros((RANK, model), F32) for _ in range(3))
+        for first_pair, end_pair in ((0, AHEAD), (AHEAD, count)):
+            here = slice(first_pair * part, end_pair * part)
+            size = (end_pair - first_pair) * part
+            gzu = jnp.zeros((size, RANK), F32)
+            for r in range(nh):
+
+                def down(c, carry, r=r, here=here):
+                    cols = window(c, chunk)
+                    df = nt(gf[here], wd[r, cols, :]) + nn(gzd[here], bt[inner_at(0, r), cols])
+                    slope[r, here, cols] = (df * slope[r, here, cols].astype(F32)).astype(BF16)
+                    return carry
+
+                lax.fori_loop(0, model // chunk, down, 0, unroll=True)
+                ga = slope[r, here]
+                gzu = gzu + nt(ga, bt[inner_at(1, r), :])
+                term = nt(ga, wu[r])
+                if r == 0:
+                    acc[here] = r2[here] + term
+                else:
+                    acc[here] += term
+            gzu = (gzu * LOWRANK).astype(BF16)
+            g4 = g4 + tn(gzu, h1b[here])
+            e = (acc[here] + nn(gzu, p4t)) * gains[0:1]
+            gat[here] = norm_back(e, n1[here], i1[here]).astype(BF16)
+            gzo = (nt(gat[here], p8t) * LOWRANK).astype(BF16)
+            go[:, here] = (nt(wo[...], gat[here]) + nt(p3, gzo)).astype(BF16)
+            if first_pair == 0:
+                for s in range(AHEAD):
+                    for r in (2, 3, 1):
+                        send_go(r, s).start()
+                    keep_go(s).start()
+            g8 = g8 + tn(z_o[here], gat[here]) * LOWRANK
+            g3 = g3 + tn(gzo, ocat[here])
         give_gat = pltpu.make_async_copy(gat, gat_out, store.at[1])
         give_gat.start()
-        gzo = (nt(gat[...], p8t) * LOWRANK).astype(BF16)
-        go[...] = (nt(wo[...], gat[...]) + nt(p3, gzo)).astype(BF16)
-        give_go = pltpu.make_async_copy(go, go_out, store.at[2])
+        rest = pl.ds(AHEAD * part, (count - AHEAD) * part)
+        give_go = pltpu.make_async_copy(go.at[:, rest], go_out, store.at[2])
         give_go.start()
-        g8 = tn(z_o, gat[...]) * LOWRANK
-        g3 = tn(gzo, ocat[...])
+        for r in range(nh):
+            gbt[inner_at(1, r), :] = tn(z_up, slope[r]) * LOWRANK
         zeros = jnp.zeros((4 * RANK, model), F32)
         grads[0] = jnp.concatenate([g3, g4, g8, g9, zeros], axis=0).T
         grads[1] = gbt[...].T
@@ -595,6 +630,10 @@
         for w in range(3):
             sibling_own(w).wait_send()
             sibling_far(w).wait_send()
+        for s in range(AHEAD):
+            keep_go(s).wait()
+            for r in range(1, nh):
+                send_go(r, s).wait()
         for give in (give_result, give_gat, give_go, give_grads):
             give.wait()
 
@@ -610,7 +649,7 @@
     part = keys // nh
     tokens = count * part
     rows = adapters_m.shape[2]
-    padded = -(-rows // 8) * 8
+    padded, padded_more = (-(-k * rows // 16) * 16 for k in (1, 2))
     shape = jax.ShapeDtypeStruct
     dma = pltpu.SemaphoreType.DMA
     return pl.pallas_call(
@@ -628,7 +667,7 @@
             pl.BlockSpec((1, heads, keys, keys), lambda s: (s, 0, 0, 0)),
             pl.BlockSpec((1, heads, keys), lambda s: (s, 0, 0)),
             vmem(), vmem(),
-            anywhere(), anywhere(), anywhere(), anywhere(),
+            anywhere(), anywhere(), anywhere(), anywhere(), anywhere(),
         ],
         out_shape=[
             shape((count, tall, keys), BF16),
@@ -638,13 +677,15 @@
             shape((LANES, width), BF16),
             shape((count, part, model), BF16),
             shape((tokens, model), BF16),
-            shape((model, tokens), BF16),
+            shape((model, (count - AHEAD) * part), BF16),
             shape((2, model, LANES), F32),
+            shape((AHEAD, width, keys), BF16),
         ],
         scratch_shapes=[
-            pltpu.VMEM((3, padded, LANES), F32),
-            pltpu.VMEM((nh, nd, 1, padded, LANES), F32),
-            pltpu.VMEM((nh, nd, 2, padded, LANES), F32),
+            pltpu.VMEM((padded, LANES), BF16),
+            pltpu.VMEM((padded_more, LANES), BF16),
+            pltpu.VMEM((nh, nd, padded, LANES), BF16),
+            pltpu.VMEM((nh, nd, padded_more, LANES), BF16),
             pltpu.VMEM((count, width, keys), BF16),
             pltpu.VMEM((model, 8), F32),
             pltpu.VMEM((model, LANES), F32),
@@ -674,6 +715,7 @@
             dma((nh, count)), dma((nh, count)), dma((count,)),
             dma((5, 5)), dma((5, 5)), dma((2, 3)), dma((2, 3)),
             dma((4,)), dma((4,)),
+            dma((nh, AHEAD)), dma((nh, AHEAD)), dma((AHEAD,)),
         ],
         compiler_params=pltpu.CompilerParams(
             collective_id=1, has_side_effects=True, vmem_limit_bytes=VMEM_LIMIT
@@ -686,10 +728,10 @@
 
 
 def attend_back_kernel(
-    nd, nh, x_ref, proj_ref, p_ref, inv_ref, go, first, early, wt, down_t,
-    roots_m, roots_i, roots_r,
+    nd, nh, x_ref, proj_ref, p_ref, inv_ref, go, got_ready, first_hbm, early, wt, down_t,
+    roots_m_hbm, roots_i_hbm, roots_r,
     grad_in, gradients, step_m, step_i, squares,
-    got_all, gproj, grad_t, late, whole_buf, near, far, last, blocks, mixed, sq, sq_head, sq_dp,
+    roots_m, roots_i, first, load, got_all, gproj, grad_t, late, whole_buf, near, far, last, blocks, mixed, sq, sq_head, sq_dp,
     send_g, recv_g, keep_g, send_n, recv_n, send_f, recv_f,
     send_a, recv_a, send_b, recv_b, *rest,
 ):
@@ -705,10 +747,16 @@
     def at(b):
         return (d, jnp.bitwise_xor(h, b))
 
+    def fetch(w):
+        source, target = (
+            (roots_i_hbm, roots_i), (roots_m_hbm, roots_m), (first_hbm, first)
+        )[w]
+        return pltpu.make_async_copy(source, target, load.at[w])
+
     def block_of(r, s):
         return go.at[
             pl.ds(pl.multiple_of(relative[r] * width, width), width),
-            pl.ds(pl.multiple_of(s * part, part), part),
+            pl.ds((s - AHEAD) * part, part),
         ]
 
     def place_of(r, s):
@@ -725,6 +773,8 @@
         )
 
     def keep(s):
+        if s < AHEAD:
+            return pltpu.make_async_copy(got_ready.at[s], got_all.at[s], keep_g.at[s])
         return pltpu.make_async_copy(block_of(0, s), place_of(0, s), keep_g.at[s])
 
     def to_near(i, s):
@@ -756,16 +806,19 @@
         greet_signal(nd, nh)
         for s in range(count):
             keep(s).start()
+        for w in range(3):
+            fetch(w).start()
         grad_t[...] = jnp.zeros_like(grad_t)
-        greet_wait(nd, nh)
-        for s in range(count):
-            for r in (2, 3, 1):
-                bring(r, s).start()
-        two.start(early[...])
-
-    keep(step).wait()
-    for r in range(1, nh):
-        brought(r, step).wait_recv()
+
+    for s in range(count):
+
+        @pl.when(step == s)
+        def _(s=s):
+            keep(s).wait()
+            if s >= AHEAD:
+                for r in range(1, nh):
+                    brought(r, s).wait_recv()
+
     got = got_all.at[step]
     scale = jnp.asarray(DH ** (-0.5), BF16)
     for head in range(width // DH):
@@ -785,17 +838,18 @@
         gproj[part_h] = nn(kt, gst).astype(BF16)
         gproj[rows_k] = nt(qt, gst).astype(BF16)
         gproj[rows_v] = nt(gs, et).astype(BF16)
-        if head == 0:
-
-            @pl.when(step == 2)
-            def _():
-                two.over_head(0)
-
-        if head == 1:
-
-            @pl.when(step >= 1)
-            def _():
-                pass_far(jnp.maximum(step - 1, 0))
+
+    @pl.when(step == 0)
+    def _():
+        greet_wait(nd, nh)
+        for s in range(AHEAD, count):
+            for r in (2, 3, 1):
+                bring(r, s).start()
+        two.start(early[...])
+
+    @pl.when(step >= 1)
+    def _():
+        pass_far(jnp.maximum(step - 1, 0))
 
     inner = []
     for j in range(3):
@@ -805,33 +859,6 @@
         inner.append(nn(down_t[(3 + j) * RANK : (4 + j) * RANK], block) * LOWRANK)
     inner = jnp.concatenate(inner, axis=0).astype(BF16)
     grad_t[0 : 3 * RANK] += nn(inner, x_ref[0])
-    whole_buf[step] = tn(gproj[...], wt[0 : 3 * width]).astype(BF16).reshape(nh, part, model)
-    to_near(1, step).start()
-    to_near(0, step).start()
-
-    @pl.when(step == 1)
-    def _():
-        two.over_dp()
-
-    @pl.when(step == 2)
-    def _():
-        two.over_head(1)
-
-    def preconditioned(j, u, where, i):
-        where[i] = u
-        sq[j : j + 1] = jnp.broadcast_to(
-            jnp.sum(jnp.sum(u * u, axis=0, keepdims=True), axis=1, keepdims=True), (1, LANES)
-        )
-
-    def mix(t):
-        mixed[t] = tn(blocks[t], gradients[t].T, HIGH).astype(BF16)
-
-    def steps_model(t):
-        for j in range(roots_m.shape[0]):
-            tile, m = slot_of(j)
-            if tile == t:
-                g = mixed[t, m * RANK : (m + 1) * RANK]
-                preconditioned(j, nt(g, roots_m[j].astype(BF16)), step_m, j)
 
     @pl.when(step == count - 1)
     def _():
@@ -842,7 +869,37 @@
         lane = lax.broadcasted_iota(jnp.int32, rows.shape, 1)
         late[0, own_rows, :] = jnp.where(lane < 3 * RANK, late[0, own_rows, :], rows)
         one.start(late[...])
-        pass_far(count - 1)
+
+    whole_buf[step] = tn(gproj[...], wt[0 : 3 * width]).astype(BF16).reshape(nh, part, model)
+    to_near(1, step).start()
+    to_near(0, step).start()
+
+    @pl.when(step == 1)
+    def _():
+        two.over_dp()
+
+    @pl.when(step == 2)
+    def _():
+        two.over_head()
+
+    def preconditioned(j, u, where, i):
+        where[i] = u
+        sq[j : j + 1] = jnp.broadcast_to(
+            jnp.sum(jnp.sum(u * u, axis=0, keepdims=True), axis=1, keepdims=True), (1, LANES)
+        )
+
+    def mix(t):
+        mixed[t] = tn(blocks[t], gradients[t].T, HIGH).astype(BF16)
+
+    def steps_model(t):
+        for j in range(roots_m.shape[0]):
+            tile, m = slot_of(j)
+            if tile == t:
+                g = mixed[t, m * RANK : (m + 1) * RANK]
+                preconditioned(j, nt(g, roots_m[j].astype(BF16)), step_m, j)
+
+    @pl.when(step == count - 1)
+    def _():
         blocks[...] = jnp.zeros_like(blocks)
         sq[...] = jnp.zeros_like(sq)
         for j in range(roots_m.shape[0]):
@@ -856,8 +913,11 @@
                     roots_m.shape[0] + q
                 ]
         one.over_dp()
+        pass_far(count - 1)
         two.finish(gradients.at[1:3])
-        one.over_head(0)
+        for w in range(3):
+            fetch(w).wait()
+        one.over_head()
         mix(1)
         mix(2)
         for q in range(2):
@@ -869,10 +929,7 @@
                     roots_i[q, :, k * model : (k + 1) * model].astype(BF16),
                 )
             preconditioned(roots_m.shape[0] + q, u, step_i, q)
-        one.over_head(1)
         steps_model(1)
-        for s in range(count):
-            complete(s)
         one.finish(gradients.at[0:1])
         mix(0)
         steps_model(0)
@@ -896,6 +953,8 @@
         sq_dp[0] = total
         for k in range(1, nd):
             sq_over_dp(k).start()
+        for s in range(count):
+            complete(s)
         for k in range(1, nd):
             sq_over_dp(k).wait_recv()
             total = total + sq_dp[k]
@@ -908,12 +967,13 @@
             to_far(s).wait_send()
             for i in range(2):
                 to_near(i, s).wait_send()
-            for r in range(1, nh):
-                bring(r, s).wait_send()
+            if s >= AHEAD:
+                for r in range(1, nh):
+                    bring(r, s).wait_send()
 
 
 def attend_back(
-    nd, nh, hidden, proj, p, inverse, go, first, early, wt, down_t, roots_m, roots_i, roots_r
+    nd, nh, hidden, proj, p, inverse, go, got, first, early, wt, down_t, roots_m, roots_i, roots_r
 ):
     count, keys, model = hidden.shape
     part, width = first.shape[1], model // nh
@@ -931,8 +991,8 @@
             pl.BlockSpec((1, tall, keys), lambda s: (s, 0, 0)),
             pl.BlockSpec((1, heads, keys, keys), lambda s: (s, 0, 0, 0)),
             pl.BlockSpec((1, heads, keys), lambda s: (s, 0, 0)),
-            anywhere(),
-            *[vmem()] * 7,
+            anywhere(), anywhere(), anywhere(), vmem(), vmem(), vmem(), anywhere(), anywhere(),
+            vmem(),
         ],
         out_specs=[vmem()] * 5,
         out_shape=[
@@ -943,6 +1003,10 @@
             shape((16, LANES), F32),
         ],
         scratch_shapes=[
+            pltpu.VMEM(roots_m.shape, F32),
+            pltpu.VMEM(roots_i.shape, F32),
+            pltpu.VMEM((count, part, model), BF16),
+            dma((3,)),
             pltpu.VMEM((count, width, keys), BF16),
             pltpu.VMEM((3 * width, keys), BF16),
             pltpu.VMEM((LANES, model), F32),
@@ -965,7 +1029,7 @@
             collective_id=2, has_side_effects=True, vmem_limit_bytes=VMEM_LIMIT
         ),
         name="attend_back",
-    )(hidden, proj, p, inverse, go, first, early, wt, down_t, roots_m, roots_i, roots_r)
+    )(hidden, proj, p, inverse, go, got, first, early, wt, down_t, roots_m, roots_i, roots_r)
 
 
 def finish_kernel(
@@ -1068,14 +1132,14 @@
     model = hidden_input.shape[2]
     turned_m = jnp.swapaxes(adapters_model, 1, 2)
     turned_i = jnp.swapaxes(adapters_inner, 1, 2)
-    proj, p, inverse, wt, down_t, result, gat, go, early = forward(
+    proj, p, inverse, wt, down_t, result, gat, go, early, got = forward(
         nd, nh, hidden_input, pair_lengths, turned_m, turned_i,
         jnp.swapaxes(query_key_value_weight, 1, 2), qkv_bias,
         output_projection_weight, up_projection_weight, down_projection_weight,
         grad_out, shifts, gains, up_bias.reshape(1, -1),
     )
     grad_in, gradients, step_m, step_i, squares = attend_back(
-        nd, nh, hidden_input, proj, p, inverse, go, gat.reshape(grad_out.shape), early, wt, down_t,
+        nd, nh, hidden_input, proj, p, inverse, go, got, gat.reshape(grad_out.shape), early, wt, down_t,
         roots_model, roots_inner, roots_rank,
     )
     grad_in, grad_m, grad_i, adapt_m, adapt_i, new_m, new_i, new_r = finish(

time: 150 us -> 141 us (0.940)
  Pallas kernels: 148 us -> 139 us
    pallas_call x1, Pallas kernels: 83 us -> 77.5 us  [forward(): pl.pallas_call(functools.partial(forward_kernel, nd, nh), grid=(count,),...]
    pallas_call x1, Pallas kernels: 59.3 us -> 56.5 us  [attend_back(): pl.pallas_call(functools.partial(attend_back_kernel, nd, nh), grid=(count...]
where the time goes in v2:
time: 141 us
  Pallas kernels  139 us (99%)
    pallas_call x1, Pallas kernels, forward(): pl.pallas_call(functools.partial(forward_kernel, nd, nh), grid=(count,),...  77.5 us
    pallas_call x1, Pallas kernels, attend_back(): pl.pallas_call(functools.partial(attend_back_kernel, nd, nh), grid=(count...  56.5 us
    pallas_call x1, Pallas kernels, finish(): pl.pallas_call(functools.partial(finish_kernel, nh, nd * nh), in_specs=[v...  5.46 us

profile of v2, /device:TPU:0, one launch (start us, length us, event | category | flops | bytes accessed | tf_op | source)
XLA Modules:
  0.0 141.1 jit_solution(13315280017463338598)
XLA Ops:
  0.6 77.5 %forward.1 = (bf16[5,624,512]{2,1,0:T(8,128)(2,1)}, bf16[5,3,512,512]{3,2,1,0:T(8,128)(2,1)}, f32[5,3,512]{2,1,0:T(4,128)}, bf16[624,768]{1,0:T(8,128)(2,1)}, bf...) custom-call(s32[5]{0:T(128)} %lengths.1, ...), custom_call_target="tpu_custom_call" | custom-call | tf_op jit(solution)/shard_map/forward/pallas_call | solution.py:655
  78.1 56.5 %attend_back.1 = (bf16[5,128,768]{2,1,0:T(8,128)(2,1)}, f32[3,768,128]{2,1,0:T(8,128)}, f32[10,16,24]{2,1,0:T(8,128)}, f32[2,16,96]{2,1,0:T(8,128)}, f32[16,128]{1,0:T(8,128)}) custom-call(bf16[5,512,768]{2,1,0:T(8,128)(2,1)} %x_ref.3, bf16[5,624,512]{2,1,0:T(8,128)(2,1)} %get-tuple-element.33.proj_ref, bf16[5,3,512,512]{3,2,1,0:T(8,128)(2,1)} %get-tuple-element.34.p_ref, ...), custom_call_target="tpu_custom_call" | custom-call | tf_op jit(solution)/shard_map/attend_back/pallas_call | solution.py:986
  134.7 0.0 copy-start
  134.7 5.5 %finish.1 = (bf16[5,128,768]{2,1,0:T(8,128)(2,1)}, f32[10,16,24]{2,1,0:T(8,128)}, f32[2,16,96]{2,1,0:T(8,128)}, f32[10,16,24]{2,1,0:T(8,128)}, f32[2,16,96]{2,1,...) custom-call(bf16[5,128,768]{2,1,0:T(8,128)(2,1)} %get-tuple-element.42.grad_in, ...), custom_call_target="tpu_custom_call" | custom-call | tf_op jit(solution)/shard_map/finish/pallas_call | solution.py:1089
  140.1 0.0 copy-done
  140.1 0.9 copy.29
Async XLA Ops:
  134.7 5.5 %copy-start = (bf16[5,128,768]{2,1,0:T(8,128)(2,1)S(1)}, bf16[5,128,768]{2,1,0:T(8,128)(2,1)}, u32[]{:S(2)}) copy-start(bf16[5,128,768]{2,1,0:T(8,128)(2,1)} %get-tuple-element.64) | copy-start | bytes 2949124

commit v3 on v2

--- a/solution.py
+++ b/solution.py
@@ -567,6 +567,9 @@
                 keep_g.at[s],
             )
 
+        give_gat = pltpu.make_async_copy(gat, gat_out, store.at[1])
+        rest = pl.ds(AHEAD * part, (count - AHEAD) * part)
+        give_go = pltpu.make_async_copy(go.at[:, rest], go_out, store.at[2])
         g3, g4, g8 = (jnp.zeros((RANK, model), F32) for _ in range(3))
         for first_pair, end_pair in ((0, AHEAD), (AHEAD, count)):
             here = slice(first_pair * part, end_pair * part)
@@ -599,13 +602,11 @@
                     for r in (2, 3, 1):
                         send_go(r, s).start()
                     keep_go(s).start()
+            else:
+                give_gat.start()
+                give_go.start()
             g8 = g8 + tn(z_o[here], gat[here]) * LOWRANK
             g3 = g3 + tn(gzo, ocat[here])
-        give_gat = pltpu.make_async_copy(gat, gat_out, store.at[1])
-        give_gat.start()
-        rest = pl.ds(AHEAD * part, (count - AHEAD) * part)
-        give_go = pltpu.make_async_copy(go.at[:, rest], go_out, store.at[2])
-        give_go.start()
         for r in range(nh):
             gbt[inner_at(1, r), :] = tn(z_up, slope[r]) * LOWRANK
         zeros = jnp.zeros((4 * RANK, model), F32)

time: 141 us -> 141 us (level)
  no operation moved by 1% of the time
where the time goes in v3:
time: 141 us
  Pallas kernels  139 us (99%)
    pallas_call x1, Pallas kernels, forward(): pl.pallas_call(functools.partial(forward_kernel, nd, nh), grid=(count,),...  77.5 us
    pallas_call x1, Pallas kernels, attend_back(): pl.pallas_call(functools.partial(attend_back_kernel, nd, nh), grid=(count...  56.5 us
    pallas_call x1, Pallas kernels, finish(): pl.pallas_call(functools.partial(finish_kernel, nh, nd * nh), in_specs=[v...  5.46 us

profile of v3, /device:TPU:0, one launch (start us, length us, event | category | flops | bytes accessed | tf_op | source)
XLA Modules:
  0.0 141.1 jit_solution(13315280017463338598)
XLA Ops:
  0.6 77.5 %forward.1 = (bf16[5,624,512]{2,1,0:T(8,128)(2,1)}, bf16[5,3,512,512]{3,2,1,0:T(8,128)(2,1)}, f32[5,3,512]{2,1,0:T(4,128)}, bf16[624,768]{1,0:T(8,128)(2,1)}, bf...) custom-call(s32[5]{0:T(128)} %lengths.1, ...), custom_call_target="tpu_custom_call" | custom-call | tf_op jit(solution)/shard_map/forward/pallas_call | solution.py:656
  78.1 56.5 %attend_back.1 = (bf16[5,128,768]{2,1,0:T(8,128)(2,1)}, f32[3,768,128]{2,1,0:T(8,128)}, f32[10,16,24]{2,1,0:T(8,128)}, f32[2,16,96]{2,1,0:T(8,128)}, f32[16,128]{1,0:T(8,128)}) custom-call(bf16[5,512,768]{2,1,0:T(8,128)(2,1)} %x_ref.3, bf16[5,624,512]{2,1,0:T(8,128)(2,1)} %get-tuple-element.33.proj_ref, bf16[5,3,512,512]{3,2,1,0:T(8,128)(2,1)} %get-tuple-element.34.p_ref, ...), custom_call_target="tpu_custom_call" | custom-call | tf_op jit(solution)/shard_map/attend_back/pallas_call | solution.py:987
  134.7 0.0 copy-start
  134.7 5.5 %finish.1 = (bf16[5,128,768]{2,1,0:T(8,128)(2,1)}, f32[10,16,24]{2,1,0:T(8,128)}, f32[2,16,96]{2,1,0:T(8,128)}, f32[10,16,24]{2,1,0:T(8,128)}, f32[2,16,96]{2,1,...) custom-call(bf16[5,128,768]{2,1,0:T(8,128)(2,1)} %get-tuple-element.42.grad_in, ...), custom_call_target="tpu_custom_call" | custom-call | tf_op jit(solution)/shard_map/finish/pallas_call | solution.py:1090
  140.1 0.0 copy-done
  140.1 0.9 copy.29
Async XLA Ops:
  134.7 5.5 %copy-start = (bf16[5,128,768]{2,1,0:T(8,128)(2,1)S(1)}, bf16[5,128,768]{2,1,0:T(8,128)(2,1)}, u32[]{:S(2)}) copy-start(bf16[5,128,768]{2,1,0:T(8,128)(2,1)} %get-tuple-element.64) | copy-start | bytes 2949124
